TPU v7x, 32 devices: a whole 2x2x4 slice. The times are simulated.
32 devices in a mesh: member: 4 (over y, core), dp: 8 (over z, x).
Axes of the slice: x: 2, y: 2, z: 4, core: 2. Of those that a mesh axis runs over, the one named last changes fastest.
Arguments:
- states: float32 [8192, 17], P('dp'), may hold values from -6 to 6
- actions: float32 [8192, 6], P('dp'), may hold values from -0.95 to 0.95
- rewards: float32 [8192], P('dp'), may hold values from -6 to 6
- next_states: float32 [8192, 17], P('dp'), may hold values from -6 to 6
- terminal: int32 [8192], P('dp'), may hold values 0 or 1
- valid_rows: int32 [8192], P('dp'), may hold values from 0 to 1
- noise_seeds: int32 [8192, 2], P('dp'), may hold values from 0 to 255
- member_live: int32 [8], P('member'), may hold values from 0 to 1, as said below
- critic_body: float32 [8, 538, 256], P('member'), may hold values from -0.75 to 0.75
- critic_body_mom: float32 [8, 538, 256], P('member'), may hold values from -0.0048828125 to 0.0048828125
- critic_body_sq: float32 [8, 538, 256], P('member'), may hold values from 8.044036e-07 to 3.2176144e-06
- critic_body_tgt: float32 [8, 538, 256], P('member'), may hold values from -0.75 to 0.75
- critic_head: float32 [8, 257], P('member'), may hold values from -0.375 to 0.375
- critic_head_mom: float32 [8, 257], P('member'), may hold values from -0.0390625 to 0.0390625
- critic_head_sq: float32 [8, 257], P('member'), may hold values from 5.148183e-05 to 0.00020592732
- critic_head_tgt: float32 [8, 257], P('member'), may hold values from -0.375 to 0.375
- policy_body: float32 [532, 256], replicated, may hold values from -0.75 to 0.75
- policy_body_mom: float32 [532, 256], replicated, may hold values from -0.0048828125 to 0.0048828125
- policy_body_sq: float32 [532, 256], replicated, may hold values from 8.044036e-07 to 3.2176144e-06
- policy_head: float32 [257, 12], replicated, may hold values from -0.375 to 0.375
- policy_head_mom: float32 [257, 12], replicated, may hold values from -0.0390625 to 0.0390625
- policy_head_sq: float32 [257, 12], replicated, may hold values from 5.148183e-05 to 0.00020592732
- log_temp: float32 [1], replicated, may hold values from -2 to -0.5
- log_temp_mom: float32 [1], replicated, may hold values from -0.05 to 0.05
- log_temp_sq: float32 [1], replicated, may hold values from 0.001 to 0.004
Outputs:
- loss_parts: float32 [5], replicated
- grad_norm: float32 [1], replicated
- critic_body_new: float32 [8, 538, 256], P('member')
- critic_body_mom_new: float32 [8, 538, 256], P('member')
- critic_body_sq_new: float32 [8, 538, 256], P('member')
- critic_body_tgt_new: float32 [8, 538, 256], P('member')
- critic_body_half: bfloat16 [8, 538, 256], P('member')
- critic_head_new: float32 [8, 257], P('member')
- critic_head_mom_new: float32 [8, 257], P('member')
- critic_head_sq_new: float32 [8, 257], P('member')
- critic_head_tgt_new: float32 [8, 257], P('member')
- critic_head_half: bfloat16 [8, 257], P('member')
- policy_body_new: float32 [532, 256], replicated
- policy_body_mom_new: float32 [532, 256], replicated
- policy_body_sq_new: float32 [532, 256], replicated
- policy_body_half: bfloat16 [532, 256], replicated
- policy_head_new: float32 [257, 12], replicated
- policy_head_mom_new: float32 [257, 12], replicated
- policy_head_sq_new: float32 [257, 12], replicated
- policy_head_half: bfloat16 [257, 12], replicated
- log_temp_new: float32 [1], replicated
- log_temp_mom_new: float32 [1], replicated
- log_temp_sq_new: float32 [1], replicated
Inputs may be any that keep to these rules, and one draw needn't show every extreme that they name: `member_live`: in each group of 2 consecutive slots the first k are 1 and the rest 0, k from 1 to 2; some group has all 2.
All inputs are finite; a program needn't handle non-finite values. No bound on the sum of `terminal` on one device may be relied on, other than what follows from the above.
Results may differ from a plain program's by a relative error of at most 0.001.
Values sent between devices are 32-bit elements; how exact they have to be, the bound alone decides.
No kernel may reach another device: no remote copies, remote signals or barrier semaphores. Data moves between devices by JAX's collectives and lax.ppermute only.
A program may use at most 64 MiB of HBM per device.

v0:
```python
import functools

import jax
import jax.numpy as jnp
from jax import lax
from jax.experimental import pallas as pl
from jax.experimental.pallas import tpu as pltpu
from jax.sharding import PartitionSpec as P

STEPS_DONE = 5
DISCOUNT = 0.99
POLYAK_RATE = 0.005
ENTROPY_TARGET = -6.0
DIVERSITY_WEIGHT = 1.0
LEARN_RATE = 0.05
BETA_ONE = 0.5
BETA_TWO = 0.5
DECAY_RATE = 0.01
ADAM_EPSILON = 1e-08
GRAD_FLOOR = 0.0001
CLIP_NORM = 1.0
LOGSTD_LOW = -5.0
LOGSTD_HIGH = 2.0
LOG_TWO = 0.6931471805599453
HALF_LOG_TWOPI = 0.9189385332046727
FAR_VALUE = 1e30

F32 = jnp.float32
BF16 = jnp.bfloat16
HID = 256
S_DIM = 17
A_DIM = 6
X_DIM = S_DIM + A_DIM
TWO = X_DIM + 1
THREE = TWO + HID + 1
BODY = THREE + HID + 1
CRITIC_ROWS = 544
P_TWO = 24
P_THREE = 288
P_LAST = 544
P_HEAD = 552
POLICY_ROWS = 576
BLOCK = 272
VMEM = pl.BlockSpec(memory_space=pltpu.VMEM)
SMEM = pl.BlockSpec(memory_space=pltpu.SMEM)
HBM = pl.BlockSpec(memory_space=pltpu.HBM)


def call(kernel, outs, in_specs, scratch=(), us=1.0, out_specs=None, limit=32):
    return pl.pallas_call(
        kernel,
        out_shape=outs,
        in_specs=in_specs,
        out_specs=out_specs or jax.tree.map(lambda _: VMEM, outs),
        scratch_shapes=list(scratch),
        compiler_params=pltpu.CompilerParams(vmem_limit_bytes=limit * 2**20),
        cost_estimate=pl.CostEstimate(flops=int(us * 1.15e9), bytes_accessed=0, transcendentals=0),
    )


def buffers(*arrays):
    return [pltpu.VMEM(a.shape, a.dtype) for a in arrays] + [pltpu.SemaphoreType.DMA((len(arrays),))]


def start_copies(sources, targets, sem):
    copies = [pltpu.make_async_copy(a, b, sem.at[i]) for i, (a, b) in enumerate(zip(sources, targets))]
    for copy in copies:
        copy.start()
    return copies


def shape(*dims, dtype=F32):
    return jax.ShapeDtypeStruct(dims, dtype)


def dot(a, b):
    return lax.dot_general(a, b, (((1,), (0,)), ((), ())), preferred_element_type=F32)


def dot_rows(a, b):
    return lax.dot_general(a, b, (((1,), (1,)), ((), ())), preferred_element_type=F32)


def halves(w):
    high = w.astype(BF16)
    return high, (w - high.astype(F32)).astype(BF16)


def stack_weights(w):
    high = (0.5 * w).astype(BF16).astype(F32)
    return jnp.concatenate([high, high, 0.5 * w - high], axis=0).T.astype(BF16)


def stack_inputs(v):
    high = v.astype(BF16).astype(F32)
    return jnp.concatenate([high, v - high, high], axis=0).astype(BF16)


def act(z):
    t = jnp.tanh(z)
    return z + z * t, t


def slope(h, t):
    return (1.0 + h) + t * (1.0 - h)


def curve(z, t):
    return (1.0 - t * t) * (1.0 - z * t)


def wide(column):
    return jnp.broadcast_to(column, (column.shape[0], 128))


def spread(column, rows):
    return jnp.concatenate([column] * (rows // 128), axis=1)


def action_rows(v):
    k = lax.broadcasted_iota(jnp.int32, v.shape, 0)
    return jnp.where((k >= 1) & (k <= A_DIM), v, 0.0)


def row_at(v, k, like):
    return jnp.where(lax.broadcasted_iota(jnp.int32, like.shape, 0) == k, v, like)


def lane_row(block):
    return jnp.concatenate([block[i : i + 1] for i in range(block.shape[0])], axis=1)


def interleave(*streams):
    results, active = [None] * len(streams), list(enumerate(streams))
    while active:
        left = []
        for i, stream in active:
            try:
                next(stream)
                left.append((i, stream))
            except StopIteration as end:
                results[i] = end.value
        active = left
    return results


def critic_rows(ref, c):
    def read(a, b):
        return jnp.concatenate([ref[pl.ds(4 * a + 2 * t + c, b - a, stride=4), :] for t in range(2)], axis=1)

    return read


def load_trunk(body, n_in, one, mats, bias, i, backward=False):
    one[i] = stack_weights(body(0, n_in + 1))
    yield
    for k, start in enumerate((n_in + 1, n_in + 2 + HID)):
        high, low = halves(0.5 * body(start, start + HID))
        mats[i, 4 * k] = high.T
        mats[i, 4 * k + 1] = low.T
        if backward:
            mats[i, 4 * k + 2] = high
            mats[i, 4 * k + 3] = low
        bias[i, k] = wide(0.5 * body(start + HID, start + HID + 1).T)
        yield


def trunk_arrays(n, n_in):
    return [shape(n, HID, 3 * (n_in + 1), dtype=BF16), shape(n, 8, HID, HID, dtype=BF16), shape(n, 2, HID, 128)]


def trunk_scratch(n, n_in):
    return [pltpu.VMEM(a.shape, a.dtype) for a in trunk_arrays(n, n_in)]


def times(w, k, h):
    mats, i = w
    return dot(mats[i, k], h) + dot(mats[i, k + 1], h)


def times_exact(w, k, h):
    mats, i = w
    high, low = halves(h)
    return dot(mats[i, k], high) + dot(mats[i, k + 1], high) + dot(mats[i, k], low)


def policy_head_rows(turned):
    one = jnp.zeros((1, HID + 1), F32)
    return jnp.concatenate([one, turned[:A_DIM], one, one, turned[A_DIM:], one], axis=0)


def noise_of(seed_row):
    k = lax.broadcasted_iota(jnp.int32, (8, seed_row.shape[1]), 0).astype(F32) - 1.0
    return 1.7 * jnp.sin(0.618034 * seed_row + 2.39996 * k)


def actor_stream(one, mats, bias, head, head_bias, x, noise):
    rows = x.shape[1]
    z = dot(one[0], stack_inputs(x))
    yield
    z = times((mats, 0), 0, act(z)[0].astype(BF16))
    yield
    z = times((mats, 0), 4, act(z + spread(bias[0, 0], rows))[0].astype(BF16))
    yield
    high, low = halves(act(z + spread(bias[0, 1], rows))[0])
    out = dot(head, high)
    out = out[:16] + out[16:] + dot(head[:16], low) + spread(head_bias, rows)
    yield
    mean, raw = out[:8], out[8:]
    turned = jnp.tanh(raw)
    log_std = LOGSTD_LOW + 0.5 * (LOGSTD_HIGH - LOGSTD_LOW) * (turned + 1.0)
    deviation = jnp.exp(log_std) * noise
    u = mean + deviation
    soft = jnp.maximum(-2.0 * u, 0.0) + jnp.log(1.0 + jnp.exp(-jnp.abs(2.0 * u)))
    squash = 2.0 * (LOG_TWO - u - soft)
    terms = -0.5 * noise * noise - log_std - HALF_LOG_TWOPI - squash
    log_prob = jnp.sum(action_rows(terms), axis=0, keepdims=True)
    return jnp.tanh(u), turned, deviation, log_prob


def first_kernel(place, out):
    out[...] = jnp.full(out.shape, (place[0] == 0).astype(F32))


def actor_kernel(
    first, states, actions, next_states, seeds, rewards, terminal, valid, body, head, log_temp, xs, xn, xp, aux, one, mats, bias
):
    rows = states.shape[1]
    ones = jnp.ones((1, rows), F32)
    for x, source in ((xs, states), (xn, next_states), (xp, states)):
        x[0:S_DIM, :] = source[...]
        x[X_DIM : X_DIM + 1, :] = ones
    xs[S_DIM:X_DIM, :] = actions[...]
    seed = seeds[...].astype(F32)
    loading = load_trunk(lambda a, b: body[a:b], S_DIM, one, mats, bias, 0, backward=True)
    next(loading)
    head_rows = policy_head_rows(head[...])
    head_w, head_b = jnp.concatenate(halves(head_rows[:, :HID]), axis=0), wide(head_rows[:, HID:])
    carry = 1.0 - lane_row(terminal[...].astype(F32))
    temper = jnp.exp(log_temp[0])
    now_in = jnp.concatenate([states[...], ones], axis=0)
    later_in = jnp.concatenate([next_states[...], ones], axis=0)
    half = rows // 2
    done = interleave(
        *[
            actor_stream(one, mats, bias, head_w, head_b, x[:, i : i + half], noise_of(seed[k : k + 1, i : i + half]))
            for i in (0, half)
            for x, k in ((later_in, 1), (now_in, 0))
        ],
        loading,
    )[:-1]
    later = [jnp.concatenate(v, axis=1) for v in zip(*done[0::2])]
    now = [jnp.concatenate(v, axis=1) for v in zip(*done[1::2])]
    xn[S_DIM:X_DIM, :] = later[0][1 : 1 + A_DIM]
    aux[0:1, :] = lane_row(rewards[...]) - DISCOUNT * carry * temper * later[3]
    aux[1:2, :] = DISCOUNT * carry
    aux[2:3, :] = lane_row(valid[...].astype(F32))
    action, turned, deviation, log_prob = now
    xp[S_DIM:X_DIM, :] = action[1 : 1 + A_DIM]
    aux[3:4, :] = log_prob
    aux[4:5, :] = spread(first[0:1], rows)
    aux[5:8, :] = jnp.zeros((3, rows), F32)
    aux[8:16, :] = action_rows(action)
    aux[16:24, :] = action_rows(turned)
    aux[24:32, :] = action_rows(deviation)


def head_column(head, c):
    row = head[pl.ds(c, 1), :]
    return row[:, :HID].T, row[:, HID:]


def inner_rows(read):
    return jnp.concatenate(halves(0.5 * read(16, 24)), axis=0)


def action_gradient(inner, y):
    grad = dot(inner, y)
    return action_rows(grad[:8] + grad[8:])


def data_stream(one, mats, bias, i, column, inner, x, save):
    rows, w = x.shape[1], (mats, i)
    z = dot(one[i], x)
    save(0, z)
    yield
    h, t = act(z)
    d1 = slope(h, t)
    z = times_exact(w, 0, h)
    yield
    z = z + spread(bias[i, 0], rows)
    save(1, z)
    h, t = act(z)
    d2 = slope(h, t)
    z = times_exact(w, 4, h)
    yield
    z = z + spread(bias[i, 1], rows)
    save(2, z)
    h, t = act(z)
    c = times(w, 6, (spread(column, rows) * slope(h, t)).astype(BF16))
    yield
    save(3, c)
    c = times(w, 2, (c * d2).astype(BF16))
    yield
    save(4, c)
    grad = action_gradient(inner, (c * d1).astype(BF16))
    yield
    size = jnp.sum(grad * grad, axis=0, keepdims=True) + GRAD_FLOOR
    return grad * lax.rsqrt(size)


def target_stream(one, mats, bias, i, column, last, x):
    rows, w = x.shape[1], (mats, i)
    z = dot(one[i], x)
    yield
    z = times(w, 0, act(z)[0].astype(BF16))
    yield
    z = times(w, 4, act(z + spread(bias[i, 0], rows))[0].astype(BF16))
    yield
    h = act(z + spread(bias[i, 1], rows))[0]
    return jnp.sum(spread(column, rows) * h, axis=0, keepdims=True) + last


def chosen_stream(one, mats, bias, i, column, last, inner, x):
    rows = x.shape[1]
    z = dot(one[i], x)
    yield
    h, t = act(z)
    d1 = slope(h, t)
    z = dot(mats[i, 0], h.astype(BF16))
    yield
    h, t = act(z + spread(bias[i, 0], rows))
    d2 = slope(h, t)
    z = dot(mats[i, 4], h.astype(BF16))
    yield
    h, t = act(z + spread(bias[i, 1], rows))
    column = spread(column, rows)
    q = jnp.sum(column * h, axis=0, keepdims=True) + last
    c = dot(mats[i, 6], (column * slope(h, t)).astype(BF16))
    yield
    c = dot(mats[i, 2], (c * d2).astype(BF16))
    yield
    return q, action_gradient(inner, (c * d1).astype(BF16))


def critic_kernel(live, place, xs, xn, xp, body, head, body_tgt, head_tgt, out, saved, *refs):
    mine, scratch, columns = refs[:3], refs[3:6], refs[6]
    order = [place[1], 1 - place[1]]
    lasts, inners, trunks, loading = [], [], [], []
    for i in range(4):
        c = order[i % 2]
        read = critic_rows((body, body_tgt)[i // 2], c)
        trunks.append((*mine, 0) if i == 0 else (*scratch, i - 1))
        loading.append(load_trunk(read, X_DIM, *trunks[i], backward=i < 2))
        next(loading[-1])
        column, last = head_column((head, head_tgt)[i // 2], c)
        columns[i] = wide(column)
        lasts.append(last)
        if i < 2:
            inners.append(inner_rows(read))
    alive = [live[c].astype(F32) for c in order]
    rows = xs.shape[1]
    step = 256
    for start in range(0, rows, step):
        at = slice(start, start + step)
        data, later, chosen = stack_inputs(xs[:, at]), stack_inputs(xn[:, at]), stack_inputs(xp[:, at])

        def save(k, value, at=at):
            saved[k, :, at] = value

        done = interleave(
            data_stream(*trunks[0], columns[0], inners[0], data, save),
            data_stream(*trunks[1], columns[1], inners[1], data, lambda k, value: None),
            *[chosen_stream(*trunks[c], columns[c], lasts[c], inners[c], chosen) for c in range(2)],
            *[target_stream(*trunks[2 + c], columns[2 + c], lasts[2 + c], later) for c in range(2)],
            *loading,
        )
        loading = []
        unit, now, value = done[0:2], done[2:4], done[4:6]
        lowest = [jnp.where(alive[c] > 0, value[c], FAR_VALUE) for c in range(2)]
        total_n, total_q, total_g = [alive[0] * a + alive[1] * b for a, b in (unit, *zip(*now))]
        out[0:8, at] = row_at(jnp.minimum(lowest[0], lowest[1]), 7, row_at(alive[0] + alive[1], 0, total_n))
        out[8:16, at] = row_at(total_q, 0, total_g)


def merge(a, b):
    k = lax.broadcasted_iota(jnp.int32, a.shape, 0)
    return jnp.where(k == 7, jnp.minimum(a, b), a + b)


def joint_kernel(mine, other, aux, log_temp, sx, gx, sums):
    both = merge(mine[...], other[...])
    unit, grad = both[:8], both[8:]
    mask, log_prob = aux[2:3, :], aux[3:4, :]
    members = both[0:1]
    target = aux[0:1, :] + aux[1:2, :] * both[7:8]
    unit = action_rows(unit)
    sx[...] = row_at(target, 7, row_at(mask, 0, mask * unit))
    gx[...] = row_at(members, 7, grad)
    temper = jnp.exp(log_temp[0])
    spread = jnp.sum(mask * (jnp.sum(unit * unit, axis=0, keepdims=True) - members), axis=1, keepdims=True)
    actor = jnp.sum(mask * (temper * log_prob - both[8:9] / members), axis=1, keepdims=True)
    entropy = jnp.sum(mask * (log_prob + ENTROPY_TARGET), axis=1, keepdims=True)
    count = jnp.sum(mask, axis=1, keepdims=True)
    lane = lax.broadcasted_iota(jnp.int32, (1, 128), 1)
    row = jnp.where(lane == 1, spread, 0.0) + jnp.where(lane == 2, actor, 0.0)
    row = row + jnp.where(lane == 3, entropy, 0.0) + jnp.where(lane == 4, count, 0.0)
    sums[...] = row * aux[4:5, 0:128]


def policy_stream(one, mats, bias, head_back, x, rows8, by_log):
    rows, w = x.shape[1], (mats, 0)
    z = dot(one[0], stack_inputs(x))
    yield
    h, t = act(z)
    d1, h1 = slope(h, t), h.astype(BF16)
    z = times(w, 0, h1)
    yield
    h, t = act(z + spread(bias[0, 0], rows))
    d2, h2 = slope(h, t), h.astype(BF16)
    z = times(w, 4, h2)
    yield
    h, t = act(z + spread(bias[0, 1], rows))
    action, turned, deviation, by_action = rows8
    by_u = by_action * (1.0 - action * action) + by_log * 2.0 * action
    by_std = by_u * deviation - by_log
    by_raw = action_rows(by_std * (0.5 * (LOGSTD_HIGH - LOGSTD_LOW)) * (1.0 - turned * turned))
    by_out = jnp.concatenate([action_rows(by_u), by_raw], axis=0)
    high, low = halves(by_out)
    f3 = (dot(head_back, jnp.concatenate([high, low, high], axis=0)) * slope(h, t)).astype(BF16)
    yield
    f2 = (times(w, 6, f3) * d2).astype(BF16)
    yield
    f1 = (times(w, 2, f2) * d1).astype(BF16)
    yield
    return h1, h2, h.astype(BF16), f1, f2, f3, high, low, by_out


def policy_kernel(place, xs, aux, gx, one, mats, bias, head, log_temp, keep, give, full):
    rows = xs.shape[1]
    n = S_DIM
    head_high, head_low = halves(0.5 * policy_head_rows(head[...])[:, :HID])
    head_back = jnp.concatenate([head_high, head_high, head_low], axis=0).astype(F32).T.astype(BF16)
    x = row_at(1.0, n, xs[...])
    mask, members = aux[2:3, :], gx[7:8, :]
    by_action = -(mask / members) * action_rows(gx[...])
    by_log = jnp.exp(log_temp[0]) * mask
    rows8 = (aux[8:16, :], aux[16:24, :], aux[24:32, :], by_action)
    step = rows // 4
    cut = lambda v, i: v[:, i * step : (i + 1) * step]
    streams = [
        policy_stream(one, mats, bias, head_back, cut(x[: n + 1], i), [cut(v, i) for v in rows8], cut(by_log, i))
        for i in range(4)
    ]
    h1, h2, h3, f1, f2, f3, high, low, by_out = [jnp.concatenate(v, axis=1) for v in zip(*interleave(*streams))]
    ones = row_at(1.0, 0, jnp.zeros((16, rows), F32)).astype(BF16)
    start = jnp.where(lax.broadcasted_iota(jnp.int32, x.shape, 0) <= n, x, 0.0).astype(BF16)
    full[0:P_TWO, :] = dot_rows(start, f1)
    full[P_TWO:P_THREE, :] = dot_rows(jnp.concatenate([h1, ones], axis=0), f2)[: HID + 8]
    layer = dot_rows(jnp.concatenate([h2, ones], axis=0), f3)
    full[P_THREE : P_THREE + HID, :] = layer[:HID]
    last = wide(jnp.sum(by_out, axis=1, keepdims=True)).T[0:1]
    last = jnp.concatenate([last, jnp.zeros((1, HID - 16), F32)], axis=1)
    full[P_LAST:P_HEAD, :] = row_at(last, 1, layer[HID : HID + 8])
    by_head = dot_rows(jnp.concatenate([high, low], axis=0), h3)
    full[P_HEAD : P_HEAD + 16, :] = by_head[:16] + by_head[16:]
    full[P_HEAD + 16 :, :] = jnp.zeros((full.shape[0] - P_HEAD - 16, HID), F32)
    size = keep.shape[0]
    for out, x in ((keep, place[1]), (give, 1 - place[1])):
        out[...] = full[pl.ds(pl.multiple_of((2 * place[0] + x) * size, 8), size), :]


def second_stream(
    one, mats, bias, column, last, inner, inner_stack, alive, weight, x, s, saved, here, left3, here3, there3, left2, here2,
    there2, left1, right1,
):
    rows, w = x.shape[1], (mats, 0)
    total = left3.shape[1] // 2
    there = slice(total + here.start, total + here.stop)
    one_row = row_at(1.0, 0, jnp.zeros((16, rows), F32))
    none = jnp.zeros((16, rows), BF16)
    mask, target = s[0:1], s[7:8]
    left1[:, here] = jnp.concatenate([x, jnp.zeros((8, rows), F32)], axis=0).astype(BF16)
    for left in (left2, left3):
        left[HID : HID + 16, here] = one_row.astype(BF16)
        left[HID : HID + 16, there] = none
    z = dot(one[0], stack_inputs(x)) if saved is None else saved[0]
    yield
    h, t = act(z)
    d1, e1 = slope(h, t), curve(z, t)
    left2[0:HID, here] = h.astype(BF16)
    if saved is None:
        z = times_exact(w, 0, h)
        yield
        z = z + spread(bias[0, 0], rows)
    else:
        z = saved[1]
        yield
    h, t = act(z)
    d2, e2 = slope(h, t), curve(z, t)
    left3[0:HID, here] = h.astype(BF16)
    if saved is None:
        z = times_exact(w, 4, h)
        yield
        z = z + spread(bias[0, 1], rows)
    else:
        z = saved[2]
        yield
    h, t = act(z)
    d3, e3 = slope(h, t), curve(z, t)
    column = spread(column, rows)
    q = jnp.sum(column * h, axis=0, keepdims=True) + last
    miss = q - target
    half_a = alive * mask * miss
    td = jnp.sum(half_a * miss, axis=1, keepdims=True)
    head = (2.0 * half_a) * h
    b3 = column * d3
    e3 = column * e3
    cut = b3.astype(BF16)
    there3[:, here] = cut
    c2 = times(w, 6, cut) if saved is None else saved[3]
    yield
    b2 = c2 * d2
    e2 = c2 * e2
    cut = b2.astype(BF16)
    there2[:, here] = cut
    c1 = times(w, 2, cut) if saved is None else saved[4]
    yield
    b1 = c1 * d1
    e1 = c1 * e1
    cut = b1.astype(BF16)
    right1[:, there] = cut
    grad = action_gradient(inner, cut)
    yield
    size = jnp.sum(grad * grad, axis=0, keepdims=True) + GRAD_FLOOR
    cot = action_rows(s) * weight
    along = jnp.sum(grad * cot, axis=0, keepdims=True)
    v = lax.rsqrt(size) * (cot - grad * (along / size))
    left1[:, there] = jnp.concatenate(
        [jnp.zeros((16, rows), F32), 0.5 * v, jnp.zeros((8, rows), F32)], axis=0
    ).astype(BF16)
    t1 = dot(inner_stack, stack_inputs(v))
    yield
    cut = (d1 * t1).astype(BF16)
    left2[0:HID, there] = cut
    t2 = times(w, 0, cut)
    yield
    cut = (d2 * t2).astype(BF16)
    left3[0:HID, there] = cut
    t3 = times(w, 4, cut)
    yield
    head = head + d3 * t3
    head = sum(head[:, i : i + 128] for i in range(0, rows, 128))
    r = e3 * t3
    here3[:, here] = (half_a * b3 + r).astype(BF16)
    r = dot(mats[0, 6], r.astype(BF16)) * d2 + e2 * t2
    yield
    here2[:, here] = (half_a * b2 + r).astype(BF16)
    r = dot(mats[0, 2], r.astype(BF16)) * d1 + e1 * t1
    yield
    right1[:, here] = (half_a * b1 + r).astype(BF16)
    return td, jnp.sum(half_a, axis=1, keepdims=True), head


def second_kernel(live, place, xs, xs_far, sx, sx_far, gx, saved, one, mats, bias, body, head, *refs):
    (grads, sums), scratch = refs[:2], refs[2:]
    left3, here3, there3, left2, here2, there2, left1, right1 = scratch
    rows = xs.shape[1]
    mine = place[1]
    alive = jnp.where(mine == 0, live[0], live[1]).astype(F32)
    read = critic_rows(body, mine)
    column, last = head_column(head, mine)
    column = wide(column)
    inner, inner_stack = inner_rows(read), stack_weights(read(16, 24))
    weight = 2.0 * DIVERSITY_WEIGHT * alive / (gx[7:8, :] - 1.0)
    td = bias_sum = jnp.zeros((1, 1), F32)
    step = rows // 2
    by_head = jnp.zeros((HID, 128), F32)
    for td_part, bias_part, head_part in interleave(
        *[
            second_stream(
                one, mats, bias, column, last, inner, inner_stack, alive, weight[:, start : start + step],
                x[:, start : start + step], s[:, start : start + step],
                None if i else [saved[k, :, start : start + step] for k in range(5)],
                slice(i * rows + start, i * rows + start + step), *scratch,
            )
            for start in range(0, rows, step)
            for i, (x, s) in enumerate(((xs, sx), (xs_far, sx_far)))
        ]
    ):
        td, bias_sum, by_head = td + td_part, bias_sum + bias_part, by_head + head_part

    def layer(left, here, there):
        n = here.shape[1]
        return dot_rows(left[:, 0:n], here[...]) + 0.5 * dot_rows(left[:, n:], there[...])

    grads[0:TWO, :] = dot_rows(right1[...], left1[...]).T[0:TWO]
    grads[TWO:THREE, :] = layer(left2, here2, there2)[0 : HID + 1]
    grads[THREE:BODY, :] = layer(left3, here3, there3)[0 : HID + 1]
    grads[BODY : BODY + 1, :] = jnp.sum(by_head.T, axis=0, keepdims=True)
    lane = lax.broadcasted_iota(jnp.int32, (1, HID), 1)
    grads[BODY + 1 : BODY + 2, :] = jnp.where(lane == 0, 2.0 * bias_sum, 0.0)
    grads[BODY + 2 :, :] = jnp.zeros((grads.shape[0] - BODY - 2, HID), F32)
    sums[...] = jnp.where(lax.broadcasted_iota(jnp.int32, (1, 128), 1) == 0, td, 0.0)


def deal_kernel(place, critic, keep, got, *out):
    n = len(out)
    part = critic.shape[0] // n
    policy = keep[...] + got[...]
    for k in range(n):
        to = jnp.bitwise_xor(place[2], k)
        out[k][0:part, :] = critic[pl.ds(pl.multiple_of(to * part, 8), part), :]
        out[k][part:, :] = policy


def reduce_kernel(part, place, one, two, *refs):
    ins, (out, sums) = refs[:-2], refs[-2:]
    total = ins[0][...]
    for r in ins[1:]:
        total = total + r[...]
    out[...] = total
    critic, policy = total[:part], total[part:]
    square = jnp.sum(jnp.sum(critic * critic, axis=0, keepdims=True), axis=1, keepdims=True)
    once = (place[2] == 0).astype(F32)
    square = square + once * jnp.sum(jnp.sum(policy * policy, axis=0, keepdims=True), axis=1, keepdims=True)
    lane = lax.broadcasted_iota(jnp.int32, (1, 128), 1)
    row = one[...] + two[...] + jnp.where(lane == 5, square, 0.0)
    sums[...] = jnp.broadcast_to(row, sums.shape)


def piece_kernel(whole, out):
    out[...] = whole[0 : out.shape[0], :]


def adam(weights, moment, second, grads):
    moment_new = BETA_ONE * (moment + grads)
    second_new = BETA_TWO * (second + grads * grads)
    root = (1.0 / (1.0 - BETA_TWO**STEPS_DONE)) ** 0.5
    bottom = (root * second_new) * lax.rsqrt(second_new) + ADAM_EPSILON
    guess = pltpu.reciprocal(bottom, approx=True)
    inverse = guess * (2.0 - bottom * guess)
    step = ((LEARN_RATE / (1.0 - BETA_ONE**STEPS_DONE)) * moment_new) * inverse
    return (1.0 - LEARN_RATE * DECAY_RATE) * weights - step, moment_new, second_new


def scalars_kernel(log_temp, log_mom, log_sq, sums, loss, norm_out, lt, lm, ls, scale):
    total = jnp.sum(sums[...], axis=0, keepdims=True)
    entropy, count = total[:, 3:4], total[:, 4:5]
    grad_temp = -entropy / count
    norm = jnp.sqrt(total[:, 5:6] / (count * count) + grad_temp * grad_temp)
    factor = CLIP_NORM / jnp.maximum(norm, CLIP_NORM)
    lane = lax.broadcasted_iota(jnp.int32, (1, 128), 1)
    loss[...] = jnp.where(lane == 3, -log_temp[0] * entropy, total)[:, 0:5]
    norm_out[...] = norm
    one = lambda v: jnp.full((1, 1), v[0])
    put((lt, lm, ls), (slice(0, 1),), adam(one(log_temp), one(log_mom), one(log_sq), factor * grad_temp))
    scale[...] = jnp.broadcast_to(factor / count, (8, 128))


def put(refs, at, got):
    for r, value in zip(refs, got):
        r[at] = value.astype(r.dtype)


def update_kernel(n_z, part, small, sources, n_pieces, n_blocks, place, scale, *refs):
    refs = list(refs)
    take = lambda n: [refs.pop(0) for _ in range(n)]
    pieces, blocks = take(n_pieces), take(n_blocks)
    w, m, v, t, hw, hm, hv, ht, pw, pm, pv, phw, phm, phv = take(14)
    outs = take(18)
    total, policy = take(2)
    near, sem, body_sem = take(18), *take(2)
    scale = scale[0:1, 0:1]
    for k, i, first, start, stop in sources:
        piece = pieces[i]
        c = jnp.bitwise_xor(place[1], k // n_z)
        z = jnp.bitwise_xor(place[2], k % n_z)
        for side in range(2):
            at = pl.ds(4 * (part * z + start) + 2 * side + c, stop - start, stride=4)
            total[at, :] = piece[first : first + stop - start, side * 128 : (side + 1) * 128]
    copies = []

    def send(i, j):
        copies.extend(start_copies(near[i:j], outs[i:j], sem.at[pl.ds(i, j - i)]))

    rows = w.shape[0]
    step = BLOCK
    for i, start in enumerate(range(0, rows, step)):
        at = pl.ds(start, min(step, rows - start))
        new, mom, sq = adam(w[at, :], m[at, :], v[at, :], total[at, :] * scale)
        tgt = t[at, :] + POLYAK_RATE * (new - t[at, :])
        put(near[0:5], (at, slice(None)), (new, mom, sq, tgt, new))
        copies += start_copies([r.at[at, :] for r in near[0:4]], [r.at[at, :] for r in outs[0:4]], body_sem.at[i])
    send(4, 5)
    for c in range(2):
        at = slice(c, c + 1)
        rows8 = [total[4 * (BODY + k) + 2 * side + c : 4 * (BODY + k) + 2 * side + c + 1, :] for k, side in ((0, 0), (0, 1), (1, 0))]
        grad = jnp.concatenate([rows8[0], rows8[1], rows8[2][:, 0:1]], axis=1)
        new, mom, sq = adam(hw[at, :], hm[at, :], hv[at, :], grad * scale)
        tgt = ht[at, :] + POLYAK_RATE * (new - ht[at, :])
        put(near[5:10], (at, slice(None)), (new, mom, sq, tgt, new))
    send(5, 10)
    first = 0
    for block in blocks:
        for k in range(block.shape[0] // small):
            at = 2 * jnp.bitwise_xor(place[0], first + k // 2) + jnp.bitwise_xor(place[1], k % 2)
            policy[pl.ds(pl.multiple_of(at * small, 8), small), :] = block[k * small : (k + 1) * small, :]
        first += block.shape[0] // (2 * small)
    n = S_DIM
    for mine, at in (
        (slice(0, n + 1), slice(0, n + 1)),
        (slice(P_TWO, P_TWO + HID + 1), slice(n + 1, n + 2 + HID)),
        (slice(P_THREE, P_THREE + HID + 1), slice(n + 2 + HID, n + 3 + 2 * HID)),
    ):
        new, mom, sq = adam(pw[at], pm[at], pv[at], policy[mine, :] * scale)
        put(near[10:14], (at,), (new, mom, sq, new))
    send(10, 14)
    by_head = policy[P_HEAD : P_HEAD + 16, :]
    last = jnp.broadcast_to(policy[P_LAST + 1 : P_LAST + 2, 0:16], (8, 16)).T[:, 0:1]
    for r, at in ((1, slice(0, A_DIM)), (9, slice(A_DIM, 2 * A_DIM))):
        grad = jnp.concatenate([by_head[r : r + A_DIM], last[r : r + A_DIM]], axis=1)
        new, mom, sq = adam(phw[at, :], phm[at, :], phv[at, :], grad * scale)
        put(near[14:18], (at, slice(None)), (new, mom, sq, new))
    send(14, 18)
    for copy in copies:
        copy.wait()


def join_kernel(n, plan, *refs):
    for out, slices in zip(refs[n:], plan):
        at = 0
        for i, start, stop in slices:
            out[at : at + stop - start, :] = refs[i][start:stop, :]
            at += stop - start


def join(arrays, plan):
    outs = [shape(sum(stop - start for _, start, stop in slices), HID) for slices in plan]
    return call(functools.partial(join_kernel, len(arrays), plan), outs, [VMEM] * len(arrays), us=0.3)(*arrays)


def flat(v):
    return jnp.transpose(v.reshape(2, -1, 2, 128), (1, 2, 0, 3)).reshape(-1, 128)


def unflat(v):
    return jnp.transpose(v.reshape(-1, 2, 2, 128), (2, 0, 1, 3)).reshape(2, -1, HID)


def per_device(
    members,
    dp,
    states,
    actions,
    rewards,
    next_states,
    terminal,
    valid_rows,
    noise_seeds,
    member_live,
    critic_body,
    critic_body_mom,
    critic_body_sq,
    critic_body_tgt,
    critic_head,
    critic_head_mom,
    critic_head_sq,
    critic_head_tgt,
    policy_body,
    policy_body_mom,
    policy_body_sq,
    policy_head,
    policy_head_mom,
    policy_head_sq,
    log_temp,
    log_temp_mom,
    log_temp_sq,
):
    rows = states.shape[0]
    n_z = dp // 2
    part = -(-CRITIC_ROWS // (8 * n_z)) * 8
    small = -(-POLICY_ROWS // (16 * members)) * 8
    m, d = lax.axis_index("member"), lax.axis_index("dp")
    place = jnp.stack([m, d // n_z, d % n_z]).astype(jnp.int32)

    def across(value, axis, n, to):
        return lax.ppermute(value, axis, [(i, to(i)) for i in range(n)])

    def to_member(value, bit):
        return across(value, "member", members, lambda i: i ^ bit)

    def to_pair(value):
        return across(value, "dp", dp, lambda i: i ^ n_z)

    def along(value, offset):
        return across(value, "dp", dp, lambda i: i ^ offset)

    square = lambda v: v.reshape(rows // 128, 128)
    turned = [policy_head.T, policy_head_mom.T, policy_head_sq.T]
    body, mom, sq, body_tgt = flat(critic_body), flat(critic_body_mom), flat(critic_body_sq), flat(critic_body_tgt)
    like = lambda *arrays: [shape(*a.shape, dtype=a.dtype) for a in arrays]
    first = call(first_kernel, shape(8, 128), [SMEM], us=8.0, limit=1)(place)
    xs, xn, xp, aux, *actor_weights = call(
        actor_kernel,
        [shape(24, rows), shape(24, rows), shape(24, rows), shape(32, rows)] + trunk_arrays(1, S_DIM),
        [VMEM] * 10 + [SMEM],
        us=3.0,
    )(
        first, states.T, actions.T, next_states.T, noise_seeds.T, square(rewards), square(terminal), square(valid_rows),
        policy_body, turned[0], log_temp,
    )
    xs_far = to_pair(xs)
    ensemble, saved, *weights = call(
        critic_kernel,
        [shape(16, rows), shape(5, HID, rows)] + trunk_arrays(1, X_DIM),
        [SMEM, SMEM] + [VMEM] * 7,
        trunk_scratch(3, X_DIM) + [pltpu.VMEM((4, HID, 128), F32)],
        us=8.0,
    )(
        member_live, place, xs, xn, xp, body, critic_head, body_tgt, critic_head_tgt
    )
    bit = 1
    while bit * 2 < members:
        other = to_member(ensemble, bit)
        k = lax.broadcasted_iota(jnp.int32, ensemble.shape, 0)
        ensemble = jnp.where(k == 7, jnp.minimum(ensemble, other), ensemble + other)
        bit *= 2
    sx, gx, sums_joint = call(
        joint_kernel, [shape(8, rows), shape(8, rows), shape(1, 128)], [VMEM, VMEM, VMEM, SMEM], us=0.7
    )(ensemble, to_member(ensemble, bit), aux, log_temp)
    sx_far = to_pair(sx)
    keep, give = call(
        policy_kernel,
        [shape(small, HID), shape(small, HID)],
        [SMEM] + [VMEM] * 7 + [SMEM],
        [pltpu.VMEM((2 * members * small, HID), F32)],
        us=3.0,
    )(place, xs, aux, gx, *actor_weights, turned[0], log_temp)
    got = to_pair(give)
    both = 2 * rows
    left, side = pltpu.VMEM((HID + 16, 2 * both), BF16), pltpu.VMEM((HID, both), BF16)
    scratch = [left, side, side, left, side, side]
    scratch = scratch + [pltpu.VMEM((32, 2 * both), BF16), pltpu.VMEM((HID, 2 * both), BF16)]
    grads, sums_second = call(
        second_kernel,
        [shape(part * n_z, HID), shape(1, 128)],
        [SMEM, SMEM] + [VMEM] * 11,
        scratch,
        us=8.0,
        limit=42,
    )(member_live, place, xs, xs_far, sx, sx_far, gx, saved, *weights, body, critic_head)
    message = shape(part + small, HID)
    dealt = call(deal_kernel, [message] * n_z, [SMEM, VMEM, VMEM, VMEM], us=0.5)(place, grads, keep, got)
    arrived = [dealt[0]] + [along(dealt[k], k) for k in range(1, n_z)]
    whole, sums = call(
        functools.partial(reduce_kernel, part),
        [message, shape(members * dp, 128)],
        [SMEM] + [VMEM] * (2 + n_z),
    )(place, sums_joint, sums_second, *arrived)
    sums = lax.all_to_all(sums, ("member", "dp"), 0, 0, tiled=True)
    piece = call(piece_kernel, shape(part, HID), [VMEM], us=8.0)(whole)
    pieces, bit = {0: piece, n_z: to_pair(whole)}, 1
    while bit < n_z:
        pieces[bit] = along(piece, bit)
        bit *= 2
    at_hand = sorted(pieces)
    *values, sums = lax.optimization_barrier((*[pieces[k] for k in at_hand], sums))
    pieces = dict(zip(at_hand, values))
    found = {k: [(pieces[k], 0, 0, part)] for k in at_hand}
    actor = [[(0, part, part + small), (1, part, part + small)]]
    (block,) = join([whole, pieces[n_z]], actor)
    if dp > 2:
        found[dp - 1] = [(along(pieces[0], dp - 1), 0, 0, part)]
    bits = dp.bit_length() - 1
    for level in range(2, bits):
        paths = {}
        for k in range(dp):
            if bin(k).count("1") == level:
                low, rest = k & -k, k & (k - 1)
                cut = part // 16 * 8 if k < n_z and level == 2 else 0
                paths.setdefault(low, []).append((k, cut, part))
                if cut:
                    paths.setdefault(rest, []).append((k, 0, cut))
        inputs = sorted({k & ~bit for bit, slices in paths.items() for k, _, _ in slices})
        plan = []
        for bit, slices in paths.items():
            plan.append([])
            for k, start, stop in slices:
                first = found[k & ~bit][0][1]
                plan[-1].append((inputs.index(k & ~bit), first + start, first + stop))
        sent = join([found[k][0][0] for k in inputs], plan)
        level_found = {}
        for (bit, slices), message in zip(paths.items(), sent):
            came, at = along(message, bit), 0
            for k, start, stop in slices:
                level_found.setdefault(k, []).append((came, at, start, stop))
                at += stop - start
        if level + 1 < bits:
            whole_ones = sorted(level_found)
            rows_of = [join([v[0] for v in sorted(level_found[k], key=lambda v: v[2])], [[(i, v[1], v[1] + v[3] - v[2]) for i, v in enumerate(sorted(level_found[k], key=lambda v: v[2]))]])[0] for k in whole_ones]
            level_found = {k: [(v, 0, 0, part)] for k, v in zip(whole_ones, rows_of)}
        found.update(level_found)
    blocks = [block] + [to_member(block, k) for k in range(1, members)]
    arrays, sources = [], []
    for k, places in sorted(found.items()):
        for array, at, start, stop in places:
            if not any(array is other for other in arrays):
                arrays.append(array)
            sources.append((k, [array is other for other in arrays].index(True), at, start, stop))
    halved = lambda a: shape(*a.shape, dtype=BF16)
    heads = [critic_head, critic_head_mom, critic_head_sq, critic_head_tgt]
    single = shape(1, 1)
    loss, norm, lt_new, lt_mom, lt_sq, scale = call(
        scalars_kernel, [shape(1, 5), single, single, single, single, shape(8, 128)], [SMEM] * 3 + [VMEM], us=0.5
    )(log_temp, log_temp_mom, log_temp_sq, sums)
    outs = like(body, body, body, body) + [halved(body)] + like(*heads) + [halved(critic_head)]
    outs = outs + like(policy_body, policy_body, policy_body) + [halved(policy_body)] + like(*turned) + [halved(turned[0])]
    new = call(
        functools.partial(update_kernel, n_z, part, small, sources, len(arrays), len(blocks)),
        outs,
        [SMEM] + [VMEM] * (1 + len(arrays) + len(blocks) + 14),
        [pltpu.VMEM((4 * n_z * part, 128), F32), pltpu.VMEM((2 * members * small, HID), F32)]
        + buffers(*outs)
        + [pltpu.SemaphoreType.DMA((-(-body.shape[0] // BLOCK), 4))],
        us=5.0,
        out_specs=[HBM] * len(outs),
    )(
        place, scale, *arrays, *blocks, body, mom, sq, body_tgt, *heads, policy_body, policy_body_mom, policy_body_sq, *turned,
    )
    new = list(new)
    new = [unflat(v) for v in new[:5]] + new[5:14] + [v.T for v in new[14:]]
    return (loss[0], norm[0], *new, lt_new[0], lt_mom[0], lt_sq[0])


def solution(mesh):
    row, line = P("dp", None), P("dp")
    stack, flat = P("member", None, None), P("member", None)
    return jax.shard_map(
        functools.partial(per_device, mesh.shape["member"], mesh.shape["dp"]),
        mesh=mesh,
        in_specs=(row, row, line, row, line, line, row, P("member")) + (stack,) * 4 + (flat,) * 4 + (P(),) * 9,
        out_specs=(P(), P()) + (stack,) * 5 + (flat,) * 5 + (P(),) * 11,
        check_vma=False,
    )
```

profile of v0, /device:TPU:1, one launch (start us, length us, event | category | flops | bytes accessed | tf_op | source)
XLA Modules:
  0.0 81.4 jit_solution(8678779603744789411)
XLA Ops:
  1.5 0.5 shard_map.416.first
  2.0 0.4 copy-done.4
  2.6 2.7 %shard_map.417 = (f32[24,1024]{1,0:T(8,128)S(1)}, f32[24,1024]{1,0:T(8,128)S(1)}, f32[24,1024]{1,0:T(8,128)S(1)}, f32[32,1024]{1,0:T(8,128)S(1)}, bf16[1,256,54]...) custom-call(f32[8,128]{1,0:T(8,128)S(1)} %shard_map.416.first, ...), custom_call_target="tpu_custom_call" | custom-call | flops 3449999872 | tf_op jit(solution)/shard_map/pallas_call | solution.py:804
  5.3 8.8 %shard_map.418 = (f32[16,1024]{1,0:T(8,128)S(1)}, f32[5,256,1024]{2,1,0:T(8,128)S(1)}, bf16[1,256,72]{2,1,0:T(8,128)(2,1)S(1)}, bf16[1,8,256,256]{3,2,1,0:T(8,128)(2,1)S(1)}, f32[1,2,256,128]{3,2,1,0:T(8,128)S(1)}) custom-call(s32[2]{0:T(128)S(1)} %copy-done.21, s32[3]{0:T(128)S(1)} %pad_add_fusion.place, f32[24,1024]{1,0:T(8,128)S(1)} %get-tuple-element.79.xs, ...), custom_call_target="tpu_custom_call" | custom-call | flops 9200000000 | tf_op jit(solution)/shard_map/pallas_call | solution.py:814
  14.2 1.2 %collective-permute-done = f32[16,1024]{1,0:T(8,128)S(1)} collective-permute-done((f32[16,1024]{1,0:T(8,128)S(1)}, f32[16,1024]{1,0:T(8,128)S(1)}, u32[]{:S(2)}, u32[]{:S(2)}) %collective-permute-start) | collective-permute-done | bytes 65568 | tf_op jit(solution)/shard_map/ppermute | solution.py:788
  15.5 2.4 %collective-permute-start.1 = (f32[16,1024]{1,0:T(8,128)S(1)}, f32[16,1024]{1,0:T(8,128)S(1)}, u32[]{:S(2)}, u32[]{:S(2)}) collective-permute-start(f32[16,1024]{1,0:T(8,128)S(1)} %add_select_fusion.mine), channel_id=1, source_target_pairs={{0,16},{8,24},{16,0},{24,8},{1,17},{9,25},{17,1},{25,9},{2,18},{10... | collective-permute-start | bytes 196616 | tf_op jit(solution)/shard_map/ppermute | solution.py:788
  17.9 2.3 %collective-permute-start.2 = (f32[24,1024]{1,0:T(8,128)S(1)}, f32[24,1024]{1,0:T(8,128)S(1)}, u32[]{:S(2)}, u32[]{:S(2)}) collective-permute-start(f32[24,1024]{1,0:T(8,128)S(1)} %get-tuple-element.79.xs), channel_id=1, source_target_pairs={{0,4},{1,5},{2,6},{3,7},{4,0},{5,1},{6,2},{7,3},{8,12},{9,13},{10,... | collective-permute-start | bytes 294920 | tf_op jit(solution)/shard_map/ppermute | solution.py:788
  20.2 0.1 shard_map.419
  20.3 1.9 %collective-permute-start.3 = (f32[8,1024]{1,0:T(8,128)S(1)}, f32[8,1024]{1,0:T(8,128)S(1)}, u32[]{:S(2)}, u32[]{:S(2)}) collective-permute-start(f32[8,1024]{1,0:T(8,128)S(1)} %get-tuple-element.85.sx), channel_id=1, source_target_pairs={{0,4},{1,5},{2,6},{3,7},{4,0},{5,1},{6,2},{7,3},{8,12},{9,13},{10,... | collective-permute-start | bytes 98312 | tf_op jit(solution)/shard_map/ppermute | solution.py:788
  22.2 3.1 %shard_map.421 = (f32[72,256]{1,0:T(8,128)S(1)}, f32[72,256]{1,0:T(8,128)S(1)}) custom-call(s32[3]{0:T(128)S(1)} %pad_add_fusion.place, f32[24,1024]{1,0:T(8,128)S(1)} %get-tuple-element.79.xs, f32[32,1024]{1,0:T(8,128)S(1)} %get-tuple-element.83.aux, f32[8,1024]{1,0:T(8,128)S(1)} %get-tuple-element.86.gx, bf16[1,256,54]{2,1,0:T(8,128)(2,1)S(1)} %get-tuple-element.93.one, ...), custom_call_target="tpu_custom_call" | custom-call | flops 3449999872 | tf_op jit(solution)/shard_map/pallas_call | solution.py:833
  25.3 0.6 collective-permute-start.4
  25.9 8.8 %shard_map.420 = (f32[544,256]{1,0:T(8,128)S(1)}, f32[1,128]{1,0:T(1,128)S(1)}) custom-call(s32[2]{0:T(128)S(1)} %copy-done.21, s32[3]{0:T(128)S(1)} %pad_add_fusion.place, f32[24,1024]{1,0:T(8,128)S(1)} %get-tuple-element.79.xs, f32[24,1024]{1,0:T(8,128)S(1)} %collective-permute-done.2.xs_far, f32[8,1024]{1,0:T(8,128)S(1)} %get-tuple-element.85.sx, ...), custom_call_target="tpu_custom_call" | custom-call | flops 9200000000 | tf_op jit(solution)/shard_map/pallas_call | solution.py:845
  34.7 0.6 shard_map.422
  35.3 1.3 %collective-permute-start.5 = (f32[208,256]{1,0:T(8,128)S(1)}, f32[208,256]{1,0:T(8,128)S(1)}, u32[]{:S(2)}, u32[]{:S(2)}) collective-permute-start(f32[208,256]{1,0:T(8,128)S(1)} %get-tuple-element.99), channel_id=1, source_target_pairs={{0,1},{1,0},{2,3},{3,2},{4,5},{5,4},{6,7},{7,6},{8,9},{9,8},{10,11... | collective-permute-start | bytes 638984 | tf_op jit(solution)/shard_map/ppermute | solution.py:788
  36.5 1.5 %collective-permute-start.6 = (f32[208,256]{1,0:T(8,128)S(1)}, f32[208,256]{1,0:T(8,128)S(1)}, u32[]{:S(2)}, u32[]{:S(2)}) collective-permute-start(f32[208,256]{1,0:T(8,128)S(1)} %get-tuple-element.100), channel_id=1, source_target_pairs={{0,2},{1,3},{2,0},{3,1},{4,6},{5,7},{6,4},{7,5},{8,10},{9,11},{10,... | collective-permute-start | bytes 638984 | tf_op jit(solution)/shard_map/ppermute | solution.py:788
  38.1 2.3 %collective-permute-done.5.refs_1_ = f32[208,256]{1,0:T(8,128)S(1)} collective-permute-done((f32[208,256]{1,0:T(8,128)S(1)}, f32[208,256]{1,0:T(8,128)S(1)}, u32[]{:S(2)}, u32[]{:S(2)}) %collective-permute-start.5) | collective-permute-done | bytes 213024 | tf_op jit(solution)/shard_map/ppermute | solution.py:788
  40.4 1.2 %collective-permute-done.6.refs_2_ = f32[208,256]{1,0:T(8,128)S(1)} collective-permute-done((f32[208,256]{1,0:T(8,128)S(1)}, f32[208,256]{1,0:T(8,128)S(1)}, u32[]{:S(2)}, u32[]{:S(2)}) %collective-permute-start.6) | collective-permute-done | bytes 213024 | tf_op jit(solution)/shard_map/ppermute | solution.py:788
  41.6 4.6 %collective-permute-done.7.refs_3_ = f32[208,256]{1,0:T(8,128)S(1)} collective-permute-done((f32[208,256]{1,0:T(8,128)S(1)}, f32[208,256]{1,0:T(8,128)S(1)}, u32[]{:S(2)}, u32[]{:S(2)}) %collective-permute-start.7) | collective-permute-done | bytes 213024 | tf_op jit(solution)/shard_map/ppermute | solution.py:788
  46.2 0.7 shard_map.423
  46.9 3.7 %collective-permute-start.10 = (f32[208,256]{1,0:T(8,128)S(1)}, f32[208,256]{1,0:T(8,128)S(1)}, u32[]{:S(2)}, u32[]{:S(2)}) collective-permute-start(f32[208,256]{1,0:T(8,128)S(1)} %get-tuple-element.102.whole.refs_0_), channel_id=1, source_target_pairs={{0,4},{1,5},{2,6},{3,7},{4,0},{5,1},{6,2},{7,3},{8,12},{9,13},{10,... | collective-permute-start | bytes 638984 | tf_op jit(solution)/shard_map/ppermute | solution.py:788
  50.7 1.7 %collective-permute-start.9 = (f32[136,256]{1,0:T(8,128)S(1)}, f32[136,256]{1,0:T(8,128)S(1)}, u32[]{:S(2)}, u32[]{:S(2)}) collective-permute-start(f32[136,256]{1,0:T(8,128)S(1)} %shard_map.424.refs_0_), channel_id=1, source_target_pairs={{0,2},{1,3},{2,0},{3,1},{4,6},{5,7},{6,4},{7,5},{8,10},{9,11},{10,... | collective-permute-start | bytes 417800 | tf_op jit(solution)/shard_map/ppermute | solution.py:788
  52.4 1.2 %collective-permute-start.8 = (f32[136,256]{1,0:T(8,128)S(1)}, f32[136,256]{1,0:T(8,128)S(1)}, u32[]{:S(2)}, u32[]{:S(2)}) collective-permute-start(f32[136,256]{1,0:T(8,128)S(1)} %shard_map.424.refs_0_), channel_id=1, source_target_pairs={{0,1},{1,0},{2,3},{3,2},{4,5},{5,4},{6,7},{7,6},{8,9},{9,8},{10,11... | collective-permute-start | bytes 417800 | tf_op jit(solution)/shard_map/ppermute | solution.py:788
  53.6 10.7 %all_to_all.12 = f32[32,1,128]{2,1,0:T(1,128)S(1)} all-to-all(f32[32,1,128]{2,1,0:T(1,128)S(1)} %bitcast.72), channel_id=1, replica_groups=mesh['member'=4,'dp'=8] {'member','dp'}, dimensions={0} | all-to-all | bytes 32768 | tf_op jit(solution)/shard_map/all_to_all | solution.py:861
  64.3 1.2 %collective-permute-start.13 = (f32[136,256]{1,0:T(8,128)S(1)}, f32[136,256]{1,0:T(8,128)S(1)}, u32[]{:S(2)}, u32[]{:S(2)}) collective-permute-start(f32[136,256]{1,0:T(8,128)S(1)} %shard_map.424.refs_0_), channel_id=1, source_target_pairs={{0,7},{1,6},{2,5},{3,4},{4,3},{5,2},{6,1},{7,0},{8,15},{9,14},{10,... | collective-permute-start | bytes 417800 | tf_op jit(solution)/shard_map/ppermute | solution.py:788
  65.6 0.9 %collective-permute-start.11 = (f32[208,256]{1,0:T(8,128)S(1)}, f32[208,256]{1,0:T(8,128)S(1)}, u32[]{:S(2)}, u32[]{:S(2)}) collective-permute-start(f32[208,256]{1,0:T(8,128)S(1)} %get-tuple-element.112), channel_id=1, source_target_pairs={{0,1},{1,0},{2,3},{3,2},{4,5},{5,4},{6,7},{7,6},{8,9},{9,8},{10,11... | collective-permute-start | bytes 638984 | tf_op jit(solution)/shard_map/ppermute | solution.py:788
  66.6 2.4 %collective-permute-start.16 = (f32[144,256]{1,0:T(8,128)S(1)}, f32[144,256]{1,0:T(8,128)S(1)}, u32[]{:S(2)}, u32[]{:S(2)}) collective-permute-start(f32[144,256]{1,0:T(8,128)S(1)} %shard_map.427.refs_7_), channel_id=1, source_target_pairs={{0,24},{8,16},{16,8},{24,0},{1,25},{9,17},{17,9},{25,1},{2,26},{10... | collective-permute-start | bytes 442376 | tf_op jit(solution)/shard_map/ppermute | solution.py:788
  69.0 0.4 collective-permute-start.15
  69.4 2.4 %collective-permute-done.13.refs_6_ = f32[136,256]{1,0:T(8,128)S(1)} collective-permute-done((f32[136,256]{1,0:T(8,128)S(1)}, f32[136,256]{1,0:T(8,128)S(1)}, u32[]{:S(2)}, u32[]{:S(2)}) %collective-permute-start.13) | collective-permute-done | bytes 139296 | tf_op jit(solution)/shard_map/ppermute | solution.py:788
  71.7 2.6 %collective-permute-start.14 = (f32[144,256]{1,0:T(8,128)S(1)}, f32[144,256]{1,0:T(8,128)S(1)}, u32[]{:S(2)}, u32[]{:S(2)}) collective-permute-start(f32[144,256]{1,0:T(8,128)S(1)} %shard_map.427.refs_7_), channel_id=1, source_target_pairs={{0,8},{8,0},{16,24},{24,16},{1,9},{9,1},{17,25},{25,17},{2,10},{10... | collective-permute-start | bytes 442376 | tf_op jit(solution)/shard_map/ppermute | solution.py:788
  75.6 0.8 shard_map.425
  76.4 0.4 collective-permute-done.15.refs_9_
  76.9 4.3 %shard_map.428 = (f32[2152,128]{1,0:T(8,128)}, f32[2152,128]{1,0:T(8,128)}, f32[2152,128]{1,0:T(8,128)}, f32[2152,128]{1,0:T(8,128)}, bf16[2152,128]{1,0:T(8,128...) custom-call(s32[3]{0:T(128)S(1)} %pad_add_fusion.place, ...), custom_call_target="tpu_custom_call" | custom-call | flops 5750000128 | tf_op jit(solution)/shard_map/pallas_call | solution.py:919
  (63 shorter events, 0.5 us)
Async XLA Ops:
  1.4 1.1 %copy-start.8 = (f32[1024,17]{0,1:T(8,128)S(1)}, f32[1024,17]{0,1:T(8,128)}, u32[]{:S(2)}) copy-start(f32[1024,17]{0,1:T(8,128)} %param.28) | copy-start | bytes 208900
  1.4 1.1 %copy-start.9 = (f32[1024,6]{0,1:T(8,128)S(1)}, f32[1024,6]{0,1:T(8,128)}, u32[]{:S(2)}) copy-start(f32[1024,6]{0,1:T(8,128)} %param.26) | copy-start | bytes 73732
  2.5 2.8 %copy-start = (f32[2,538,256]{2,0,1:T(2,128)S(1)}, f32[2,538,256]{2,0,1:T(2,128)}, u32[]{:S(2)}) copy-start(f32[2,538,256]{2,0,1:T(2,128)} %param.33) | copy-start | bytes 3305476
  2.5 2.8 %copy-start.1 = (f32[2,538,256]{2,0,1:T(2,128)S(1)}, f32[2,538,256]{2,0,1:T(2,128)}, u32[]{:S(2)}) copy-start(f32[2,538,256]{2,0,1:T(2,128)} %param.36) | copy-start | bytes 3305476
  2.5 2.8 %copy-start.17 = (f32[2,257]{1,0:T(2,128)S(1)}, f32[2,257]{1,0:T(2,128)}, u32[]{:S(2)}) copy-start(f32[2,257]{1,0:T(2,128)} %refs_15_.1) | copy-start | bytes 6172
  2.6 2.7 %copy-start.18 = (f32[2,257]{1,0:T(2,128)S(1)}, f32[2,257]{1,0:T(2,128)}, u32[]{:S(2)}) copy-start(f32[2,257]{1,0:T(2,128)} %refs_18_.1) | copy-start | bytes 6172
  2.6 2.7 %copy-start.21 = (s32[2]{0:T(128)S(1)}, s32[2]{0:T(128)}, u32[]{:S(2)}) copy-start(s32[2]{0:T(128)} %live.3) | copy-start | bytes 28
  14.1 1.3 %collective-permute-start = (f32[16,1024]{1,0:T(8,128)S(1)}, f32[16,1024]{1,0:T(8,128)S(1)}, u32[]{:S(2)}, u32[]{:S(2)}) collective-permute-start(f32[16,1024]{1,0:T(8,128)S(1)} %get-tuple-element.82), channel_id=1, source_target_pairs={{0,8},{8,0},{16,24},{24,16},{1,9},{9,1},{17,25},{25,17},{2,10},{10... | collective-permute-start | bytes 196616 | tf_op jit(solution)/shard_map/ppermute | solution.py:788
  15.5 4.7 %collective-permute-start.1 = (f32[16,1024]{1,0:T(8,128)S(1)}, f32[16,1024]{1,0:T(8,128)S(1)}, u32[]{:S(2)}, u32[]{:S(2)}) collective-permute-start(f32[16,1024]{1,0:T(8,128)S(1)} %add_select_fusion.mine), channel_id=1, source_target_pairs={{0,16},{8,24},{16,0},{24,8},{1,17},{9,25},{17,1},{25,9},{2,18},{10... | collective-permute-start | bytes 196616 | tf_op jit(solution)/shard_map/ppermute | solution.py:788
  17.9 8.0 %collective-permute-start.2 = (f32[24,1024]{1,0:T(8,128)S(1)}, f32[24,1024]{1,0:T(8,128)S(1)}, u32[]{:S(2)}, u32[]{:S(2)}) collective-permute-start(f32[24,1024]{1,0:T(8,128)S(1)} %get-tuple-element.79.xs), channel_id=1, source_target_pairs={{0,4},{1,5},{2,6},{3,7},{4,0},{5,1},{6,2},{7,3},{8,12},{9,13},{10,... | collective-permute-start | bytes 294920 | tf_op jit(solution)/shard_map/ppermute | solution.py:788
  20.3 5.5 %collective-permute-start.3 = (f32[8,1024]{1,0:T(8,128)S(1)}, f32[8,1024]{1,0:T(8,128)S(1)}, u32[]{:S(2)}, u32[]{:S(2)}) collective-permute-start(f32[8,1024]{1,0:T(8,128)S(1)} %get-tuple-element.85.sx), channel_id=1, source_target_pairs={{0,4},{1,5},{2,6},{3,7},{4,0},{5,1},{6,2},{7,3},{8,12},{9,13},{10,... | collective-permute-start | bytes 98312 | tf_op jit(solution)/shard_map/ppermute | solution.py:788
  25.3 9.3 %collective-permute-start.4 = (f32[72,256]{1,0:T(8,128)S(1)}, f32[72,256]{1,0:T(8,128)S(1)}, u32[]{:S(2)}, u32[]{:S(2)}) collective-permute-start(f32[72,256]{1,0:T(8,128)S(1)} %get-tuple-element.97), channel_id=1, source_target_pairs={{0,4},{1,5},{2,6},{3,7},{4,0},{5,1},{6,2},{7,3},{8,12},{9,13},{10,... | collective-permute-start | bytes 221192 | tf_op jit(solution)/shard_map/ppermute | solution.py:788
  35.3 5.2 %collective-permute-start.5 = (f32[208,256]{1,0:T(8,128)S(1)}, f32[208,256]{1,0:T(8,128)S(1)}, u32[]{:S(2)}, u32[]{:S(2)}) collective-permute-start(f32[208,256]{1,0:T(8,128)S(1)} %get-tuple-element.99), channel_id=1, source_target_pairs={{0,1},{1,0},{2,3},{3,2},{4,5},{5,4},{6,7},{7,6},{8,9},{9,8},{10,11... | collective-permute-start | bytes 638984 | tf_op jit(solution)/shard_map/ppermute | solution.py:788
  36.5 5.1 %collective-permute-start.6 = (f32[208,256]{1,0:T(8,128)S(1)}, f32[208,256]{1,0:T(8,128)S(1)}, u32[]{:S(2)}, u32[]{:S(2)}) collective-permute-start(f32[208,256]{1,0:T(8,128)S(1)} %get-tuple-element.100), channel_id=1, source_target_pairs={{0,2},{1,3},{2,0},{3,1},{4,6},{5,7},{6,4},{7,5},{8,10},{9,11},{10,... | collective-permute-start | bytes 638984 | tf_op jit(solution)/shard_map/ppermute | solution.py:788
  38.1 8.2 %collective-permute-start.7 = (f32[208,256]{1,0:T(8,128)S(1)}, f32[208,256]{1,0:T(8,128)S(1)}, u32[]{:S(2)}, u32[]{:S(2)}) collective-permute-start(f32[208,256]{1,0:T(8,128)S(1)} %get-tuple-element.101), channel_id=1, source_target_pairs={{0,3},{1,2},{2,1},{3,0},{4,7},{5,6},{6,5},{7,4},{8,11},{9,10},{10,... | collective-permute-start | bytes 638984 | tf_op jit(solution)/shard_map/ppermute | solution.py:788
  46.9 17.4 %collective-permute-start.10 = (f32[208,256]{1,0:T(8,128)S(1)}, f32[208,256]{1,0:T(8,128)S(1)}, u32[]{:S(2)}, u32[]{:S(2)}) collective-permute-start(f32[208,256]{1,0:T(8,128)S(1)} %get-tuple-element.102.whole.refs_0_), channel_id=1, source_target_pairs={{0,4},{1,5},{2,6},{3,7},{4,0},{5,1},{6,2},{7,3},{8,12},{9,13},{10,... | collective-permute-start | bytes 638984 | tf_op jit(solution)/shard_map/ppermute | solution.py:788
  50.7 13.7 %collective-permute-start.9 = (f32[136,256]{1,0:T(8,128)S(1)}, f32[136,256]{1,0:T(8,128)S(1)}, u32[]{:S(2)}, u32[]{:S(2)}) collective-permute-start(f32[136,256]{1,0:T(8,128)S(1)} %shard_map.424.refs_0_), channel_id=1, source_target_pairs={{0,2},{1,3},{2,0},{3,1},{4,6},{5,7},{6,4},{7,5},{8,10},{9,11},{10,... | collective-permute-start | bytes 417800 | tf_op jit(solution)/shard_map/ppermute | solution.py:788
  52.4 11.9 %collective-permute-start.8 = (f32[136,256]{1,0:T(8,128)S(1)}, f32[136,256]{1,0:T(8,128)S(1)}, u32[]{:S(2)}, u32[]{:S(2)}) collective-permute-start(f32[136,256]{1,0:T(8,128)S(1)} %shard_map.424.refs_0_), channel_id=1, source_target_pairs={{0,1},{1,0},{2,3},{3,2},{4,5},{5,4},{6,7},{7,6},{8,9},{9,8},{10,11... | collective-permute-start | bytes 417800 | tf_op jit(solution)/shard_map/ppermute | solution.py:788
  64.3 7.4 %collective-permute-start.13 = (f32[136,256]{1,0:T(8,128)S(1)}, f32[136,256]{1,0:T(8,128)S(1)}, u32[]{:S(2)}, u32[]{:S(2)}) collective-permute-start(f32[136,256]{1,0:T(8,128)S(1)} %shard_map.424.refs_0_), channel_id=1, source_target_pairs={{0,7},{1,6},{2,5},{3,4},{4,3},{5,2},{6,1},{7,0},{8,15},{9,14},{10,... | collective-permute-start | bytes 417800 | tf_op jit(solution)/shard_map/ppermute | solution.py:788
  65.6 11.2 %collective-permute-start.11 = (f32[208,256]{1,0:T(8,128)S(1)}, f32[208,256]{1,0:T(8,128)S(1)}, u32[]{:S(2)}, u32[]{:S(2)}) collective-permute-start(f32[208,256]{1,0:T(8,128)S(1)} %get-tuple-element.112), channel_id=1, source_target_pairs={{0,1},{1,0},{2,3},{3,2},{4,5},{5,4},{6,7},{7,6},{8,9},{9,8},{10,11... | collective-permute-start | bytes 638984 | tf_op jit(solution)/shard_map/ppermute | solution.py:788
  66.5 10.3 %collective-permute-start.12 = (f32[200,256]{1,0:T(8,128)S(1)}, f32[200,256]{1,0:T(8,128)S(1)}, u32[]{:S(2)}, u32[]{:S(2)}) collective-permute-start(f32[200,256]{1,0:T(8,128)S(1)} %get-tuple-element.113), channel_id=1, source_target_pairs={{0,2},{1,3},{2,0},{3,1},{4,6},{5,7},{6,4},{7,5},{8,10},{9,11},{10,... | collective-permute-start | bytes 614408 | tf_op jit(solution)/shard_map/ppermute | solution.py:788
  66.5 10.3 %copy-start.3 = (f32[2,538,256]{2,0,1:T(2,128)S(1)}, f32[2,538,256]{2,0,1:T(2,128)}, u32[]{:S(2)}) copy-start(f32[2,538,256]{2,0,1:T(2,128)} %param.35) | copy-start | bytes 3305476
  66.5 10.3 %copy-start.6 = (f32[532,256]{1,0:T(8,128)S(1)}, f32[532,256]{1,0:T(8,128)}, u32[]{:S(2)}) copy-start(f32[532,256]{1,0:T(8,128)} %refs_21_.1) | copy-start | bytes 1634308
  66.5 10.3 %copy-start.2 = (f32[2,538,256]{2,0,1:T(2,128)S(1)}, f32[2,538,256]{2,0,1:T(2,128)}, u32[]{:S(2)}) copy-start(f32[2,538,256]{2,0,1:T(2,128)} %param.34) | copy-start | bytes 3305476
  66.5 10.3 %copy-start.5 = (f32[532,256]{1,0:T(8,128)S(1)}, f32[532,256]{1,0:T(8,128)}, u32[]{:S(2)}) copy-start(f32[532,256]{1,0:T(8,128)} %refs_20_.1) | copy-start | bytes 1634308
  66.6 10.3 %copy-start.11 = (f32[257,12]{0,1:T(8,128)S(1)}, f32[257,12]{0,1:T(8,128)}, u32[]{:S(2)}) copy-start(f32[257,12]{0,1:T(8,128)} %param.45) | copy-start | bytes 37012
  66.6 10.3 %copy-start.12 = (f32[257,12]{0,1:T(8,128)S(1)}, f32[257,12]{0,1:T(8,128)}, u32[]{:S(2)}) copy-start(f32[257,12]{0,1:T(8,128)} %param.46) | copy-start | bytes 37012
  66.6 10.3 %copy-start.19 = (f32[2,257]{1,0:T(2,128)S(1)}, f32[2,257]{1,0:T(2,128)}, u32[]{:S(2)}) copy-start(f32[2,257]{1,0:T(2,128)} %refs_16_.1) | copy-start | bytes 6172
  66.6 10.3 %copy-start.20 = (f32[2,257]{1,0:T(2,128)S(1)}, f32[2,257]{1,0:T(2,128)}, u32[]{:S(2)}) copy-start(f32[2,257]{1,0:T(2,128)} %refs_17_.1) | copy-start | bytes 6172
  66.6 9.8 %collective-permute-start.16 = (f32[144,256]{1,0:T(8,128)S(1)}, f32[144,256]{1,0:T(8,128)S(1)}, u32[]{:S(2)}, u32[]{:S(2)}) collective-permute-start(f32[144,256]{1,0:T(8,128)S(1)} %shard_map.427.refs_7_), channel_id=1, source_target_pairs={{0,24},{8,16},{16,8},{24,0},{1,25},{9,17},{17,9},{25,1},{2,26},{10... | collective-permute-start | bytes 442376 | tf_op jit(solution)/shard_map/ppermute | solution.py:788
  69.0 7.8 %collective-permute-start.15 = (f32[144,256]{1,0:T(8,128)S(1)}, f32[144,256]{1,0:T(8,128)S(1)}, u32[]{:S(2)}, u32[]{:S(2)}) collective-permute-start(f32[144,256]{1,0:T(8,128)S(1)} %shard_map.427.refs_7_), channel_id=1, source_target_pairs={{0,16},{8,24},{16,0},{24,8},{1,17},{9,25},{17,1},{25,9},{2,18},{10... | collective-permute-start | bytes 442376 | tf_op jit(solution)/shard_map/ppermute | solution.py:788
  71.7 5.1 %collective-permute-start.14 = (f32[144,256]{1,0:T(8,128)S(1)}, f32[144,256]{1,0:T(8,128)S(1)}, u32[]{:S(2)}, u32[]{:S(2)}) collective-permute-start(f32[144,256]{1,0:T(8,128)S(1)} %shard_map.427.refs_7_), channel_id=1, source_target_pairs={{0,8},{8,0},{16,24},{24,16},{1,9},{9,1},{17,25},{25,17},{2,10},{10... | collective-permute-start | bytes 442376 | tf_op jit(solution)/shard_map/ppermute | solution.py:788
  (7 other events, 7.4 us)
where the time goes:
time: 81.9 us; the launch traced here: 81.4 us
  Pallas kernels  30.4 us (37%)
  starting transfers between devices  24.2 us (30%)
  waiting for transfers between devices  12.2 us (15%)
  blocking collectives  10.7 us (13%)
  between operations  3.14 us (4%)
    ppermute x17, starting transfers between devices, across(): return lax.ppermute(value, axis, [(i, to(i)) for i in range(n)])  24.2 us
    ppermute x17, waiting for transfers between devices, across(): return lax.ppermute(value, axis, [(i, to(i)) for i in range(n)])  12.2 us
    all_to_all x1, blocking collectives, per_device(): sums = lax.all_to_all(sums, ('member', 'dp'), 0, 0, tiled=True)  10.7 us
    pallas_call x1, Pallas kernels, per_device(): call(critic_kernel, [shape(16, rows), shape(5, HID, rows)] + trunk_arrays...  8.79 us
    pallas_call x1, Pallas kernels, per_device(): call(second_kernel, [shape(part * n_z, HID), shape(1, 128)], [SMEM, SMEM]...  8.77 us
    pallas_call x1, Pallas kernels, per_device(): call(functools.partial(update_kernel, n_z, part, small, sources, len(arra...  4.31 us
    pallas_call x1, Pallas kernels, per_device(): call(policy_kernel, [shape(small, HID), shape(small, HID)], [SMEM] + [VME...  3.08 us
    pallas_call x1, Pallas kernels, per_device(): call(actor_kernel, [shape(24, rows), shape(24, rows), shape(24, rows), sh...  2.69 us
  transfers between devices with their start and end apart: 17, of which 6 were waited for; matrix products, arithmetic and copies ran while one was open for 0% of the time, Pallas kernels for 16%

commit v1 on v0

--- a/solution.py
+++ b/solution.py
@@ -470,9 +470,13 @@
         out[...] = full[pl.ds(pl.multiple_of((2 * place[0] + x) * size, 8), size), :]
 
 
+def padded(parts, rows):
+    return jnp.concatenate([v if n == 0 else jnp.zeros((n, rows), F32) for n, v in parts], axis=0).astype(BF16)
+
+
 def second_stream(
     one, mats, bias, column, last, inner, inner_stack, alive, weight, x, s, saved, here, left3, here3, there3, left2, here2,
-    there2, left1, right1,
+    there2,
 ):
     rows, w = x.shape[1], (mats, 0)
     total = left3.shape[1] // 2
@@ -480,7 +484,6 @@
     one_row = row_at(1.0, 0, jnp.zeros((16, rows), F32))
     none = jnp.zeros((16, rows), BF16)
     mask, target = s[0:1], s[7:8]
-    left1[:, here] = jnp.concatenate([x, jnp.zeros((8, rows), F32)], axis=0).astype(BF16)
     for left in (left2, left3):
         left[HID : HID + 16, here] = one_row.astype(BF16)
         left[HID : HID + 16, there] = none
@@ -529,16 +532,14 @@
     b1 = c1 * d1
     e1 = c1 * e1
     cut = b1.astype(BF16)
-    right1[:, there] = cut
+    there1 = cut
     grad = action_gradient(inner, cut)
     yield
     size = jnp.sum(grad * grad, axis=0, keepdims=True) + GRAD_FLOOR
     cot = action_rows(s) * weight
     along = jnp.sum(grad * cot, axis=0, keepdims=True)
     v = lax.rsqrt(size) * (cot - grad * (along / size))
-    left1[:, there] = jnp.concatenate(
-        [jnp.zeros((16, rows), F32), 0.5 * v, jnp.zeros((8, rows), F32)], axis=0
-    ).astype(BF16)
+    first = dot_rows(there1, padded([(16, 0), (0, 0.5 * v), (8, 0)], rows))
     t1 = dot(inner_stack, stack_inputs(v))
     yield
     cut = (d1 * t1).astype(BF16)
@@ -558,13 +559,13 @@
     here2[:, here] = (half_a * b2 + r).astype(BF16)
     r = dot(mats[0, 2], r.astype(BF16)) * d1 + e1 * t1
     yield
-    right1[:, here] = (half_a * b1 + r).astype(BF16)
-    return td, jnp.sum(half_a, axis=1, keepdims=True), head
+    first = first + dot_rows((half_a * b1 + r).astype(BF16), padded([(0, x), (8, 0)], rows))
+    return td, jnp.sum(half_a, axis=1, keepdims=True), head, first
 
 
 def second_kernel(live, place, xs, xs_far, sx, sx_far, gx, saved, one, mats, bias, body, head, *refs):
     (grads, sums), scratch = refs[:2], refs[2:]
-    left3, here3, there3, left2, here2, there2, left1, right1 = scratch
+    left3, here3, there3, left2, here2, there2 = scratch
     rows = xs.shape[1]
     mine = place[1]
     alive = jnp.where(mine == 0, live[0], live[1]).astype(F32)
@@ -575,8 +576,8 @@
     weight = 2.0 * DIVERSITY_WEIGHT * alive / (gx[7:8, :] - 1.0)
     td = bias_sum = jnp.zeros((1, 1), F32)
     step = rows // 2
-    by_head = jnp.zeros((HID, 128), F32)
-    for td_part, bias_part, head_part in interleave(
+    by_head, first = jnp.zeros((HID, 128), F32), jnp.zeros((HID, 32), F32)
+    for td_part, bias_part, head_part, first_part in interleave(
         *[
             second_stream(
                 one, mats, bias, column, last, inner, inner_stack, alive, weight[:, start : start + step],
@@ -588,13 +589,13 @@
             for i, (x, s) in enumerate(((xs, sx), (xs_far, sx_far)))
         ]
     ):
-        td, bias_sum, by_head = td + td_part, bias_sum + bias_part, by_head + head_part
+        td, bias_sum, by_head, first = td + td_part, bias_sum + bias_part, by_head + head_part, first + first_part
 
     def layer(left, here, there):
         n = here.shape[1]
         return dot_rows(left[:, 0:n], here[...]) + 0.5 * dot_rows(left[:, n:], there[...])
 
-    grads[0:TWO, :] = dot_rows(right1[...], left1[...]).T[0:TWO]
+    grads[0:TWO, :] = first.T[0:TWO]
     grads[TWO:THREE, :] = layer(left2, here2, there2)[0 : HID + 1]
     grads[THREE:BODY, :] = layer(left3, here3, there3)[0 : HID + 1]
     grads[BODY : BODY + 1, :] = jnp.sum(by_head.T, axis=0, keepdims=True)
@@ -663,14 +664,12 @@
         r[at] = value.astype(r.dtype)
 
 
-def update_kernel(n_z, part, small, sources, n_pieces, n_blocks, place, scale, *refs):
+def critic_update_kernel(n_z, part, sources, n_pieces, place, scale, *refs):
     refs = list(refs)
     take = lambda n: [refs.pop(0) for _ in range(n)]
-    pieces, blocks = take(n_pieces), take(n_blocks)
-    w, m, v, t, hw, hm, hv, ht, pw, pm, pv, phw, phm, phv = take(14)
-    outs = take(18)
-    total, policy = take(2)
-    near, sem, body_sem = take(18), *take(2)
+    pieces = take(n_pieces)
+    w, m, v, t, hw, hm, hv, ht = take(8)
+    outs, (total,), near, (sem, body_sem) = take(10), take(1), take(10), take(2)
     scale = scale[0:1, 0:1]
     for k, i, first, start, stop in sources:
         piece = pieces[i]
@@ -680,19 +679,14 @@
             at = pl.ds(4 * (part * z + start) + 2 * side + c, stop - start, stride=4)
             total[at, :] = piece[first : first + stop - start, side * 128 : (side + 1) * 128]
     copies = []
-
-    def send(i, j):
-        copies.extend(start_copies(near[i:j], outs[i:j], sem.at[pl.ds(i, j - i)]))
-
     rows = w.shape[0]
-    step = BLOCK
-    for i, start in enumerate(range(0, rows, step)):
-        at = pl.ds(start, min(step, rows - start))
+    for i, start in enumerate(range(0, rows, BLOCK)):
+        at = pl.ds(start, min(BLOCK, rows - start))
         new, mom, sq = adam(w[at, :], m[at, :], v[at, :], total[at, :] * scale)
         tgt = t[at, :] + POLYAK_RATE * (new - t[at, :])
         put(near[0:5], (at, slice(None)), (new, mom, sq, tgt, new))
         copies += start_copies([r.at[at, :] for r in near[0:4]], [r.at[at, :] for r in outs[0:4]], body_sem.at[i])
-    send(4, 5)
+    copies += start_copies(near[4:5], outs[4:5], sem)
     for c in range(2):
         at = slice(c, c + 1)
         rows8 = [total[4 * (BODY + k) + 2 * side + c : 4 * (BODY + k) + 2 * side + c + 1, :] for k, side in ((0, 0), (0, 1), (1, 0))]
@@ -700,29 +694,36 @@
         new, mom, sq = adam(hw[at, :], hm[at, :], hv[at, :], grad * scale)
         tgt = ht[at, :] + POLYAK_RATE * (new - ht[at, :])
         put(near[5:10], (at, slice(None)), (new, mom, sq, tgt, new))
-    send(5, 10)
-    first = 0
-    for block in blocks:
-        for k in range(block.shape[0] // small):
-            at = 2 * jnp.bitwise_xor(place[0], first + k // 2) + jnp.bitwise_xor(place[1], k % 2)
-            policy[pl.ds(pl.multiple_of(at * small, 8), small), :] = block[k * small : (k + 1) * small, :]
-        first += block.shape[0] // (2 * small)
+    copies += start_copies(near[5:], outs[5:], sem.at[pl.ds(5, 5)])
+    for copy in copies:
+        copy.wait()
+
+
+def policy_update_kernel(small, n_blocks, place, scale, *refs):
+    refs = list(refs)
+    take = lambda n: [refs.pop(0) for _ in range(n)]
+    blocks, (w, m, v, hw, hm, hv), outs, (policy,), near, (sem,) = take(n_blocks), take(6), take(8), take(1), take(8), take(1)
+    scale = scale[0:1, 0:1]
+    for owner, block in enumerate(blocks):
+        for x in range(2):
+            at = 2 * jnp.bitwise_xor(place[0], owner) + jnp.bitwise_xor(place[1], x)
+            policy[pl.ds(pl.multiple_of(at * small, 8), small), :] = block[x * small : (x + 1) * small, :]
     n = S_DIM
     for mine, at in (
         (slice(0, n + 1), slice(0, n + 1)),
         (slice(P_TWO, P_TWO + HID + 1), slice(n + 1, n + 2 + HID)),
         (slice(P_THREE, P_THREE + HID + 1), slice(n + 2 + HID, n + 3 + 2 * HID)),
     ):
-        new, mom, sq = adam(pw[at], pm[at], pv[at], policy[mine, :] * scale)
-        put(near[10:14], (at,), (new, mom, sq, new))
-    send(10, 14)
+        new, mom, sq = adam(w[at], m[at], v[at], policy[mine, :] * scale)
+        put(near[0:4], (at,), (new, mom, sq, new))
+    copies = start_copies(near[:4], outs[:4], sem)
     by_head = policy[P_HEAD : P_HEAD + 16, :]
     last = jnp.broadcast_to(policy[P_LAST + 1 : P_LAST + 2, 0:16], (8, 16)).T[:, 0:1]
     for r, at in ((1, slice(0, A_DIM)), (9, slice(A_DIM, 2 * A_DIM))):
         grad = jnp.concatenate([by_head[r : r + A_DIM], last[r : r + A_DIM]], axis=1)
-        new, mom, sq = adam(phw[at, :], phm[at, :], phv[at, :], grad * scale)
-        put(near[14:18], (at, slice(None)), (new, mom, sq, new))
-    send(14, 18)
+        new, mom, sq = adam(hw[at, :], hm[at, :], hv[at, :], grad * scale)
+        put(near[4:8], (at, slice(None)), (new, mom, sq, new))
+    copies += start_copies(near[4:], outs[4:], sem.at[pl.ds(4, 4)])
     for copy in copies:
         copy.wait()
 
@@ -841,7 +842,6 @@
     both = 2 * rows
     left, side = pltpu.VMEM((HID + 16, 2 * both), BF16), pltpu.VMEM((HID, both), BF16)
     scratch = [left, side, side, left, side, side]
-    scratch = scratch + [pltpu.VMEM((32, 2 * both), BF16), pltpu.VMEM((HID, 2 * both), BF16)]
     grads, sums_second = call(
         second_kernel,
         [shape(part * n_z, HID), shape(1, 128)],
@@ -915,21 +915,26 @@
         scalars_kernel, [shape(1, 5), single, single, single, single, shape(8, 128)], [SMEM] * 3 + [VMEM], us=0.5
     )(log_temp, log_temp_mom, log_temp_sq, sums)
     outs = like(body, body, body, body) + [halved(body)] + like(*heads) + [halved(critic_head)]
-    outs = outs + like(policy_body, policy_body, policy_body) + [halved(policy_body)] + like(*turned) + [halved(turned[0])]
-    new = call(
-        functools.partial(update_kernel, n_z, part, small, sources, len(arrays), len(blocks)),
+    critic = call(
+        functools.partial(critic_update_kernel, n_z, part, sources, len(arrays)),
         outs,
-        [SMEM] + [VMEM] * (1 + len(arrays) + len(blocks) + 14),
-        [pltpu.VMEM((4 * n_z * part, 128), F32), pltpu.VMEM((2 * members * small, HID), F32)]
+        [SMEM] + [VMEM] * (1 + len(arrays) + 8),
+        [pltpu.VMEM((4 * n_z * part, 128), F32)]
         + buffers(*outs)
         + [pltpu.SemaphoreType.DMA((-(-body.shape[0] // BLOCK), 4))],
-        us=5.0,
+        us=6.0,
         out_specs=[HBM] * len(outs),
-    )(
-        place, scale, *arrays, *blocks, body, mom, sq, body_tgt, *heads, policy_body, policy_body_mom, policy_body_sq, *turned,
-    )
-    new = list(new)
-    new = [unflat(v) for v in new[:5]] + new[5:14] + [v.T for v in new[14:]]
+    )(place, scale, *arrays, body, mom, sq, body_tgt, *heads)
+    outs = like(policy_body, policy_body, policy_body) + [halved(policy_body)] + like(*turned) + [halved(turned[0])]
+    policy = call(
+        functools.partial(policy_update_kernel, small, len(blocks)),
+        outs,
+        [SMEM] + [VMEM] * (1 + len(blocks) + 6),
+        [pltpu.VMEM((2 * members * small, HID), F32)] + buffers(*outs),
+        us=0.2,
+        out_specs=[HBM] * len(outs),
+    )(place, scale, *blocks, policy_body, policy_body_mom, policy_body_sq, *turned)
+    new = [unflat(v) for v in critic[:5]] + list(critic[5:]) + list(policy[:4]) + [v.T for v in policy[4:]]
     return (loss[0], norm[0], *new, lt_new[0], lt_mom[0], lt_sq[0])
 
 

time: 81.9 us -> 81 us (0.989)
  starting transfers between devices: 24.2 us -> 22.4 us
  Pallas kernels: 30.4 us -> 32.1 us
    ppermute x17, starting transfers between devices: 24.2 us -> 22.4 us  [across(): return lax.ppermute(value, axis, [(i, to(i)) for i in range(n)])]
    pallas_call x1 -> x2, Pallas kernels: 4.31 us -> 6.03 us  [the longest x1 3.43 us: per_device(): call(functools.partial(critic_update_kernel, n_z, part, sources, len(arra...]
  transfers between devices with their start and end apart: 17 -> 17, of which waited for: 6 -> 5; matrix products, arithmetic and copies ran while one was open for 0% -> 0% of each run, Pallas kernels for 16% -> 19%
where the time goes in v1:
time: 81 us; the launch traced here: 80.8 us
  Pallas kernels  32.1 us (40%)
  starting transfers between devices  22.4 us (28%)
  waiting for transfers between devices  12 us (15%)
  blocking collectives  10.7 us (13%)
  between operations  3.22 us (4%)
    ppermute x17, starting transfers between devices, across(): return lax.ppermute(value, axis, [(i, to(i)) for i in range(n)])  22.4 us
    ppermute x17, waiting for transfers between devices, across(): return lax.ppermute(value, axis, [(i, to(i)) for i in range(n)])  12 us
    all_to_all x1, blocking collectives, per_device(): sums = lax.all_to_all(sums, ('member', 'dp'), 0, 0, tiled=True)  10.7 us
    pallas_call x1, Pallas kernels, per_device(): call(critic_kernel, [shape(16, rows), shape(5, HID, rows)] + trunk_arrays...  8.79 us
    pallas_call x1, Pallas kernels, per_device(): call(second_kernel, [shape(part * n_z, HID), shape(1, 128)], [SMEM, SMEM]...  8.71 us
    pallas_call x1, Pallas kernels, per_device(): call(functools.partial(critic_update_kernel, n_z, part, sources, len(arra...  3.43 us
    pallas_call x1, Pallas kernels, per_device(): call(policy_kernel, [shape(small, HID), shape(small, HID)], [SMEM] + [VME...  3.09 us
    pallas_call x1, Pallas kernels, per_device(): call(actor_kernel, [shape(24, rows), shape(24, rows), shape(24, rows), sh...  2.71 us
  transfers between devices with their start and end apart: 17, of which 5 were waited for; matrix products, arithmetic and copies ran while one was open for 0% of the time, Pallas kernels for 19%

profile of v1, /device:TPU:1, one launch (start us, length us, event | category | flops | bytes accessed | tf_op | source)
XLA Modules:
  0.0 80.8 jit_solution(4308542459568682511)
XLA Ops:
  0.8 0.5 shard_map.416.first
  2.2 2.7 %shard_map.417 = (f32[24,1024]{1,0:T(8,128)S(1)}, f32[24,1024]{1,0:T(8,128)S(1)}, f32[24,1024]{1,0:T(8,128)S(1)}, f32[32,1024]{1,0:T(8,128)S(1)}, bf16[1,256,54]...) custom-call(f32[8,128]{1,0:T(8,128)S(1)} %shard_map.416.first, ...), custom_call_target="tpu_custom_call" | custom-call | flops 3449999872 | tf_op jit(solution)/shard_map/pallas_call | solution.py:805
  4.9 8.8 %shard_map.418 = (f32[16,1024]{1,0:T(8,128)S(1)}, f32[5,256,1024]{2,1,0:T(8,128)S(1)}, bf16[1,256,72]{2,1,0:T(8,128)(2,1)S(1)}, bf16[1,8,256,256]{3,2,1,0:T(8,128)(2,1)S(1)}, f32[1,2,256,128]{3,2,1,0:T(8,128)S(1)}) custom-call(s32[2]{0:T(128)S(1)} %copy-done.21, s32[3]{0:T(128)S(1)} %pad_add_fusion.place, f32[24,1024]{1,0:T(8,128)S(1)} %get-tuple-element.79.xs, ...), custom_call_target="tpu_custom_call" | custom-call | flops 9200000000 | tf_op jit(solution)/shard_map/pallas_call | solution.py:815
  13.8 1.2 %collective-permute-done = f32[16,1024]{1,0:T(8,128)S(1)} collective-permute-done((f32[16,1024]{1,0:T(8,128)S(1)}, f32[16,1024]{1,0:T(8,128)S(1)}, u32[]{:S(2)}, u32[]{:S(2)}) %collective-permute-start) | collective-permute-done | bytes 65568 | tf_op jit(solution)/shard_map/ppermute | solution.py:789
  15.1 2.4 %collective-permute-start.1 = (f32[16,1024]{1,0:T(8,128)S(1)}, f32[16,1024]{1,0:T(8,128)S(1)}, u32[]{:S(2)}, u32[]{:S(2)}) collective-permute-start(f32[16,1024]{1,0:T(8,128)S(1)} %add_select_fusion.mine), channel_id=1, source_target_pairs={{0,16},{8,24},{16,0},{24,8},{1,17},{9,25},{17,1},{25,9},{2,18},{10... | collective-permute-start | bytes 196616 | tf_op jit(solution)/shard_map/ppermute | solution.py:789
  17.5 2.3 %collective-permute-start.2 = (f32[24,1024]{1,0:T(8,128)S(1)}, f32[24,1024]{1,0:T(8,128)S(1)}, u32[]{:S(2)}, u32[]{:S(2)}) collective-permute-start(f32[24,1024]{1,0:T(8,128)S(1)} %get-tuple-element.79.xs), channel_id=1, source_target_pairs={{0,4},{1,5},{2,6},{3,7},{4,0},{5,1},{6,2},{7,3},{8,12},{9,13},{10,... | collective-permute-start | bytes 294920 | tf_op jit(solution)/shard_map/ppermute | solution.py:789
  19.8 0.1 shard_map.419
  20.0 1.9 %collective-permute-start.3 = (f32[8,1024]{1,0:T(8,128)S(1)}, f32[8,1024]{1,0:T(8,128)S(1)}, u32[]{:S(2)}, u32[]{:S(2)}) collective-permute-start(f32[8,1024]{1,0:T(8,128)S(1)} %get-tuple-element.85.sx), channel_id=1, source_target_pairs={{0,4},{1,5},{2,6},{3,7},{4,0},{5,1},{6,2},{7,3},{8,12},{9,13},{10,... | collective-permute-start | bytes 98312 | tf_op jit(solution)/shard_map/ppermute | solution.py:789
  21.8 3.1 %shard_map.421 = (f32[72,256]{1,0:T(8,128)S(1)}, f32[72,256]{1,0:T(8,128)S(1)}) custom-call(s32[3]{0:T(128)S(1)} %pad_add_fusion.place, f32[24,1024]{1,0:T(8,128)S(1)} %get-tuple-element.79.xs, f32[32,1024]{1,0:T(8,128)S(1)} %get-tuple-element.83.aux, f32[8,1024]{1,0:T(8,128)S(1)} %get-tuple-element.86.gx, bf16[1,256,54]{2,1,0:T(8,128)(2,1)S(1)} %get-tuple-element.93.one, ...), custom_call_target="tpu_custom_call" | custom-call | flops 3449999872 | tf_op jit(solution)/shard_map/pallas_call | solution.py:834
  24.9 0.6 collective-permute-start.4
  25.5 8.7 %shard_map.420 = (f32[544,256]{1,0:T(8,128)S(1)}, f32[1,128]{1,0:T(1,128)S(1)}) custom-call(s32[2]{0:T(128)S(1)} %copy-done.21, s32[3]{0:T(128)S(1)} %pad_add_fusion.place, f32[24,1024]{1,0:T(8,128)S(1)} %get-tuple-element.79.xs, f32[24,1024]{1,0:T(8,128)S(1)} %collective-permute-done.2.xs_far, f32[8,1024]{1,0:T(8,128)S(1)} %get-tuple-element.85.sx, ...), custom_call_target="tpu_custom_call" | custom-call | flops 9200000000 | tf_op jit(solution)/shard_map/pallas_call | solution.py:845
  34.2 0.6 shard_map.422
  34.8 1.3 %collective-permute-start.5 = (f32[208,256]{1,0:T(8,128)S(1)}, f32[208,256]{1,0:T(8,128)S(1)}, u32[]{:S(2)}, u32[]{:S(2)}) collective-permute-start(f32[208,256]{1,0:T(8,128)S(1)} %get-tuple-element.99), channel_id=1, source_target_pairs={{0,1},{1,0},{2,3},{3,2},{4,5},{5,4},{6,7},{7,6},{8,9},{9,8},{10,11... | collective-permute-start | bytes 638984 | tf_op jit(solution)/shard_map/ppermute | solution.py:789
  36.1 1.5 %collective-permute-start.6 = (f32[208,256]{1,0:T(8,128)S(1)}, f32[208,256]{1,0:T(8,128)S(1)}, u32[]{:S(2)}, u32[]{:S(2)}) collective-permute-start(f32[208,256]{1,0:T(8,128)S(1)} %get-tuple-element.100), channel_id=1, source_target_pairs={{0,2},{1,3},{2,0},{3,1},{4,6},{5,7},{6,4},{7,5},{8,10},{9,11},{10,... | collective-permute-start | bytes 638984 | tf_op jit(solution)/shard_map/ppermute | solution.py:789
  37.6 2.4 %collective-permute-done.5.refs_1_ = f32[208,256]{1,0:T(8,128)S(1)} collective-permute-done((f32[208,256]{1,0:T(8,128)S(1)}, f32[208,256]{1,0:T(8,128)S(1)}, u32[]{:S(2)}, u32[]{:S(2)}) %collective-permute-start.5) | collective-permute-done | bytes 213024 | tf_op jit(solution)/shard_map/ppermute | solution.py:789
  40.0 1.2 %collective-permute-done.6.refs_2_ = f32[208,256]{1,0:T(8,128)S(1)} collective-permute-done((f32[208,256]{1,0:T(8,128)S(1)}, f32[208,256]{1,0:T(8,128)S(1)}, u32[]{:S(2)}, u32[]{:S(2)}) %collective-permute-start.6) | collective-permute-done | bytes 213024 | tf_op jit(solution)/shard_map/ppermute | solution.py:789
  41.2 4.6 %collective-permute-done.7.refs_3_ = f32[208,256]{1,0:T(8,128)S(1)} collective-permute-done((f32[208,256]{1,0:T(8,128)S(1)}, f32[208,256]{1,0:T(8,128)S(1)}, u32[]{:S(2)}, u32[]{:S(2)}) %collective-permute-start.7) | collective-permute-done | bytes 213024 | tf_op jit(solution)/shard_map/ppermute | solution.py:789
  45.8 0.7 shard_map.423
  46.5 3.7 %collective-permute-start.10 = (f32[208,256]{1,0:T(8,128)S(1)}, f32[208,256]{1,0:T(8,128)S(1)}, u32[]{:S(2)}, u32[]{:S(2)}) collective-permute-start(f32[208,256]{1,0:T(8,128)S(1)} %get-tuple-element.102.whole.refs_0_), channel_id=1, source_target_pairs={{0,4},{1,5},{2,6},{3,7},{4,0},{5,1},{6,2},{7,3},{8,12},{9,13},{10,... | collective-permute-start | bytes 638984 | tf_op jit(solution)/shard_map/ppermute | solution.py:789
  50.2 1.3 %collective-permute-start.8 = (f32[136,256]{1,0:T(8,128)S(1)}, f32[136,256]{1,0:T(8,128)S(1)}, u32[]{:S(2)}, u32[]{:S(2)}) collective-permute-start(f32[136,256]{1,0:T(8,128)S(1)} %shard_map.424.refs_0_), channel_id=1, source_target_pairs={{0,1},{1,0},{2,3},{3,2},{4,5},{5,4},{6,7},{7,6},{8,9},{9,8},{10,11... | collective-permute-start | bytes 417800 | tf_op jit(solution)/shard_map/ppermute | solution.py:789
  51.5 1.6 %collective-permute-start.9 = (f32[136,256]{1,0:T(8,128)S(1)}, f32[136,256]{1,0:T(8,128)S(1)}, u32[]{:S(2)}, u32[]{:S(2)}) collective-permute-start(f32[136,256]{1,0:T(8,128)S(1)} %shard_map.424.refs_0_), channel_id=1, source_target_pairs={{0,2},{1,3},{2,0},{3,1},{4,6},{5,7},{6,4},{7,5},{8,10},{9,11},{10,... | collective-permute-start | bytes 417800 | tf_op jit(solution)/shard_map/ppermute | solution.py:789
  53.1 10.7 %all_to_all.12 = f32[32,1,128]{2,1,0:T(1,128)S(1)} all-to-all(f32[32,1,128]{2,1,0:T(1,128)S(1)} %bitcast.77), channel_id=1, replica_groups=mesh['member'=4,'dp'=8] {'member','dp'}, dimensions={0} | all-to-all | bytes 32768 | tf_op jit(solution)/shard_map/all_to_all | solution.py:861
  63.9 0.7 collective-permute-start.14
  64.7 0.4 collective-permute-start.11
  65.1 0.3 collective-permute-start.12
  65.4 0.3 collective-permute-start.15
  65.7 1.9 %collective-permute-start.16 = (f32[144,256]{1,0:T(8,128)S(1)}, f32[144,256]{1,0:T(8,128)S(1)}, u32[]{:S(2)}, u32[]{:S(2)}) collective-permute-start(f32[144,256]{1,0:T(8,128)S(1)} %shard_map.428.refs_0_), channel_id=1, source_target_pairs={{0,24},{8,16},{16,8},{24,0},{1,25},{9,17},{17,9},{25,1},{2,26},{10... | collective-permute-start | bytes 442376 | tf_op jit(solution)/shard_map/ppermute | solution.py:789
  67.6 2.1 %collective-permute-start.13 = (f32[136,256]{1,0:T(8,128)S(1)}, f32[136,256]{1,0:T(8,128)S(1)}, u32[]{:S(2)}, u32[]{:S(2)}) collective-permute-start(f32[136,256]{1,0:T(8,128)S(1)} %shard_map.424.refs_0_), channel_id=1, source_target_pairs={{0,7},{1,6},{2,5},{3,4},{4,3},{5,2},{6,1},{7,0},{8,15},{9,14},{10,... | collective-permute-start | bytes 417800 | tf_op jit(solution)/shard_map/ppermute | solution.py:789
  71.0 0.8 shard_map.425
  71.8 2.6 %collective-permute-done.16.refs_3_ = f32[144,256]{1,0:T(8,128)S(1)} collective-permute-done((f32[144,256]{1,0:T(8,128)S(1)}, f32[144,256]{1,0:T(8,128)S(1)}, u32[]{:S(2)}, u32[]{:S(2)}) %collective-permute-start.16) | collective-permute-done | bytes 147488 | tf_op jit(solution)/shard_map/ppermute | solution.py:789
  74.5 2.6 %shard_map.429 = (f32[532,256]{1,0:T(8,128)}, f32[532,256]{1,0:T(8,128)}, f32[532,256]{1,0:T(8,128)}, bf16[532,256]{1,0:T(8,128)(2,1)}, f32[12,257]{1,0:T(8,128)...) custom-call(s32[3]{0:T(128)S(1)} %pad_add_fusion.place, f32[8,128]{1,0:T(8,128)S(1)} %get-tuple-element.107.scale, ...), custom_call_target="tpu_custom_call" | custom-call | flops 230000000 | tf_op jit(solution)/shard_map/pallas_call | solution.py:929
  77.2 3.4 %shard_map.427 = (f32[2152,128]{1,0:T(8,128)}, f32[2152,128]{1,0:T(8,128)}, f32[2152,128]{1,0:T(8,128)}, f32[2152,128]{1,0:T(8,128)}, bf16[2152,128]{1,0:T(8,128...) custom-call(s32[3]{0:T(128)S(1)} %pad_add_fusion.place, ...), custom_call_target="tpu_custom_call" | custom-call | flops 6899999744 | tf_op jit(solution)/shard_map/pallas_call | solution.py:918
  (64 shorter events, 0.5 us)
Async XLA Ops:
  0.8 1.3 %copy-start.11 = (f32[1024,17]{0,1:T(8,128)S(1)}, f32[1024,17]{0,1:T(8,128)}, u32[]{:S(2)}) copy-start(f32[1024,17]{0,1:T(8,128)} %param.28) | copy-start | bytes 208900
  0.8 1.3 %copy-start.12 = (f32[1024,6]{0,1:T(8,128)S(1)}, f32[1024,6]{0,1:T(8,128)}, u32[]{:S(2)}) copy-start(f32[1024,6]{0,1:T(8,128)} %param.26) | copy-start | bytes 73732
  2.1 2.8 %copy-start.6 = (f32[2,538,256]{2,0,1:T(2,128)S(1)}, f32[2,538,256]{2,0,1:T(2,128)}, u32[]{:S(2)}) copy-start(f32[2,538,256]{2,0,1:T(2,128)} %param.33) | copy-start | bytes 3305476
  2.1 2.8 %copy-start.7 = (f32[2,538,256]{2,0,1:T(2,128)S(1)}, f32[2,538,256]{2,0,1:T(2,128)}, u32[]{:S(2)}) copy-start(f32[2,538,256]{2,0,1:T(2,128)} %param.36) | copy-start | bytes 3305476
  2.1 2.8 %copy-start.17 = (f32[2,257]{1,0:T(2,128)S(1)}, f32[2,257]{1,0:T(2,128)}, u32[]{:S(2)}) copy-start(f32[2,257]{1,0:T(2,128)} %refs_11_.1) | copy-start | bytes 6172
  2.2 2.8 %copy-start.18 = (f32[2,257]{1,0:T(2,128)S(1)}, f32[2,257]{1,0:T(2,128)}, u32[]{:S(2)}) copy-start(f32[2,257]{1,0:T(2,128)} %refs_14_.1) | copy-start | bytes 6172
  2.2 2.8 %copy-start.21 = (s32[2]{0:T(128)S(1)}, s32[2]{0:T(128)}, u32[]{:S(2)}) copy-start(s32[2]{0:T(128)} %live.3) | copy-start | bytes 28
  13.7 1.3 %collective-permute-start = (f32[16,1024]{1,0:T(8,128)S(1)}, f32[16,1024]{1,0:T(8,128)S(1)}, u32[]{:S(2)}, u32[]{:S(2)}) collective-permute-start(f32[16,1024]{1,0:T(8,128)S(1)} %get-tuple-element.82), channel_id=1, source_target_pairs={{0,8},{8,0},{16,24},{24,16},{1,9},{9,1},{17,25},{25,17},{2,10},{10... | collective-permute-start | bytes 196616 | tf_op jit(solution)/shard_map/ppermute | solution.py:789
  15.1 4.7 %collective-permute-start.1 = (f32[16,1024]{1,0:T(8,128)S(1)}, f32[16,1024]{1,0:T(8,128)S(1)}, u32[]{:S(2)}, u32[]{:S(2)}) collective-permute-start(f32[16,1024]{1,0:T(8,128)S(1)} %add_select_fusion.mine), channel_id=1, source_target_pairs={{0,16},{8,24},{16,0},{24,8},{1,17},{9,25},{17,1},{25,9},{2,18},{10... | collective-permute-start | bytes 196616 | tf_op jit(solution)/shard_map/ppermute | solution.py:789
  17.5 8.0 %collective-permute-start.2 = (f32[24,1024]{1,0:T(8,128)S(1)}, f32[24,1024]{1,0:T(8,128)S(1)}, u32[]{:S(2)}, u32[]{:S(2)}) collective-permute-start(f32[24,1024]{1,0:T(8,128)S(1)} %get-tuple-element.79.xs), channel_id=1, source_target_pairs={{0,4},{1,5},{2,6},{3,7},{4,0},{5,1},{6,2},{7,3},{8,12},{9,13},{10,... | collective-permute-start | bytes 294920 | tf_op jit(solution)/shard_map/ppermute | solution.py:789
  20.0 5.5 %collective-permute-start.3 = (f32[8,1024]{1,0:T(8,128)S(1)}, f32[8,1024]{1,0:T(8,128)S(1)}, u32[]{:S(2)}, u32[]{:S(2)}) collective-permute-start(f32[8,1024]{1,0:T(8,128)S(1)} %get-tuple-element.85.sx), channel_id=1, source_target_pairs={{0,4},{1,5},{2,6},{3,7},{4,0},{5,1},{6,2},{7,3},{8,12},{9,13},{10,... | collective-permute-start | bytes 98312 | tf_op jit(solution)/shard_map/ppermute | solution.py:789
  24.9 9.3 %collective-permute-start.4 = (f32[72,256]{1,0:T(8,128)S(1)}, f32[72,256]{1,0:T(8,128)S(1)}, u32[]{:S(2)}, u32[]{:S(2)}) collective-permute-start(f32[72,256]{1,0:T(8,128)S(1)} %get-tuple-element.97), channel_id=1, source_target_pairs={{0,4},{1,5},{2,6},{3,7},{4,0},{5,1},{6,2},{7,3},{8,12},{9,13},{10,... | collective-permute-start | bytes 221192 | tf_op jit(solution)/shard_map/ppermute | solution.py:789
  34.8 5.2 %collective-permute-start.5 = (f32[208,256]{1,0:T(8,128)S(1)}, f32[208,256]{1,0:T(8,128)S(1)}, u32[]{:S(2)}, u32[]{:S(2)}) collective-permute-start(f32[208,256]{1,0:T(8,128)S(1)} %get-tuple-element.99), channel_id=1, source_target_pairs={{0,1},{1,0},{2,3},{3,2},{4,5},{5,4},{6,7},{7,6},{8,9},{9,8},{10,11... | collective-permute-start | bytes 638984 | tf_op jit(solution)/shard_map/ppermute | solution.py:789
  36.1 5.1 %collective-permute-start.6 = (f32[208,256]{1,0:T(8,128)S(1)}, f32[208,256]{1,0:T(8,128)S(1)}, u32[]{:S(2)}, u32[]{:S(2)}) collective-permute-start(f32[208,256]{1,0:T(8,128)S(1)} %get-tuple-element.100), channel_id=1, source_target_pairs={{0,2},{1,3},{2,0},{3,1},{4,6},{5,7},{6,4},{7,5},{8,10},{9,11},{10,... | collective-permute-start | bytes 638984 | tf_op jit(solution)/shard_map/ppermute | solution.py:789
  37.6 8.2 %collective-permute-start.7 = (f32[208,256]{1,0:T(8,128)S(1)}, f32[208,256]{1,0:T(8,128)S(1)}, u32[]{:S(2)}, u32[]{:S(2)}) collective-permute-start(f32[208,256]{1,0:T(8,128)S(1)} %get-tuple-element.101), channel_id=1, source_target_pairs={{0,3},{1,2},{2,1},{3,0},{4,7},{5,6},{6,5},{7,4},{8,11},{9,10},{10,... | collective-permute-start | bytes 638984 | tf_op jit(solution)/shard_map/ppermute | solution.py:789
  46.5 17.4 %collective-permute-start.10 = (f32[208,256]{1,0:T(8,128)S(1)}, f32[208,256]{1,0:T(8,128)S(1)}, u32[]{:S(2)}, u32[]{:S(2)}) collective-permute-start(f32[208,256]{1,0:T(8,128)S(1)} %get-tuple-element.102.whole.refs_0_), channel_id=1, source_target_pairs={{0,4},{1,5},{2,6},{3,7},{4,0},{5,1},{6,2},{7,3},{8,12},{9,13},{10,... | collective-permute-start | bytes 638984 | tf_op jit(solution)/shard_map/ppermute | solution.py:789
  50.2 13.7 %collective-permute-start.8 = (f32[136,256]{1,0:T(8,128)S(1)}, f32[136,256]{1,0:T(8,128)S(1)}, u32[]{:S(2)}, u32[]{:S(2)}) collective-permute-start(f32[136,256]{1,0:T(8,128)S(1)} %shard_map.424.refs_0_), channel_id=1, source_target_pairs={{0,1},{1,0},{2,3},{3,2},{4,5},{5,4},{6,7},{7,6},{8,9},{9,8},{10,11... | collective-permute-start | bytes 417800 | tf_op jit(solution)/shard_map/ppermute | solution.py:789
  51.5 12.4 %collective-permute-start.9 = (f32[136,256]{1,0:T(8,128)S(1)}, f32[136,256]{1,0:T(8,128)S(1)}, u32[]{:S(2)}, u32[]{:S(2)}) collective-permute-start(f32[136,256]{1,0:T(8,128)S(1)} %shard_map.424.refs_0_), channel_id=1, source_target_pairs={{0,2},{1,3},{2,0},{3,1},{4,6},{5,7},{6,4},{7,5},{8,10},{9,11},{10,... | collective-permute-start | bytes 417800 | tf_op jit(solution)/shard_map/ppermute | solution.py:789
  63.9 3.7 %collective-permute-start.14 = (f32[144,256]{1,0:T(8,128)S(1)}, f32[144,256]{1,0:T(8,128)S(1)}, u32[]{:S(2)}, u32[]{:S(2)}) collective-permute-start(f32[144,256]{1,0:T(8,128)S(1)} %shard_map.428.refs_0_), channel_id=1, source_target_pairs={{0,8},{8,0},{16,24},{24,16},{1,9},{9,1},{17,25},{25,17},{2,10},{10... | collective-permute-start | bytes 442376 | tf_op jit(solution)/shard_map/ppermute | solution.py:789
  64.7 9.8 %copy-start.1 = (f32[532,256]{1,0:T(8,128)S(1)}, f32[532,256]{1,0:T(8,128)}, u32[]{:S(2)}) copy-start(f32[532,256]{1,0:T(8,128)} %refs_5_.1) | copy-start | bytes 1634308
  64.7 9.8 %copy-start.2 = (f32[532,256]{1,0:T(8,128)S(1)}, f32[532,256]{1,0:T(8,128)}, u32[]{:S(2)}) copy-start(f32[532,256]{1,0:T(8,128)} %refs_6_.1) | copy-start | bytes 1634308
  64.7 9.7 %copy-start.4 = (f32[257,12]{0,1:T(8,128)S(1)}, f32[257,12]{0,1:T(8,128)}, u32[]{:S(2)}) copy-start(f32[257,12]{0,1:T(8,128)} %param.45) | copy-start | bytes 37012
  64.7 9.7 %copy-start.5 = (f32[257,12]{0,1:T(8,128)S(1)}, f32[257,12]{0,1:T(8,128)}, u32[]{:S(2)}) copy-start(f32[257,12]{0,1:T(8,128)} %param.46) | copy-start | bytes 37012
  64.7 12.4 %collective-permute-start.11 = (f32[208,256]{1,0:T(8,128)S(1)}, f32[208,256]{1,0:T(8,128)S(1)}, u32[]{:S(2)}, u32[]{:S(2)}) collective-permute-start(f32[208,256]{1,0:T(8,128)S(1)} %get-tuple-element.112), channel_id=1, source_target_pairs={{0,1},{1,0},{2,3},{3,2},{4,5},{5,4},{6,7},{7,6},{8,9},{9,8},{10,11... | collective-permute-start | bytes 638984 | tf_op jit(solution)/shard_map/ppermute | solution.py:789
  65.1 12.0 %collective-permute-start.12 = (f32[200,256]{1,0:T(8,128)S(1)}, f32[200,256]{1,0:T(8,128)S(1)}, u32[]{:S(2)}, u32[]{:S(2)}) collective-permute-start(f32[200,256]{1,0:T(8,128)S(1)} %get-tuple-element.113), channel_id=1, source_target_pairs={{0,2},{1,3},{2,0},{3,1},{4,6},{5,7},{6,4},{7,5},{8,10},{9,11},{10,... | collective-permute-start | bytes 614408 | tf_op jit(solution)/shard_map/ppermute | solution.py:789
  65.4 6.4 %collective-permute-start.15 = (f32[144,256]{1,0:T(8,128)S(1)}, f32[144,256]{1,0:T(8,128)S(1)}, u32[]{:S(2)}, u32[]{:S(2)}) collective-permute-start(f32[144,256]{1,0:T(8,128)S(1)} %shard_map.428.refs_0_), channel_id=1, source_target_pairs={{0,16},{8,24},{16,0},{24,8},{1,17},{9,25},{17,1},{25,9},{2,18},{10... | collective-permute-start | bytes 442376 | tf_op jit(solution)/shard_map/ppermute | solution.py:789
  65.7 8.7 %collective-permute-start.16 = (f32[144,256]{1,0:T(8,128)S(1)}, f32[144,256]{1,0:T(8,128)S(1)}, u32[]{:S(2)}, u32[]{:S(2)}) collective-permute-start(f32[144,256]{1,0:T(8,128)S(1)} %shard_map.428.refs_0_), channel_id=1, source_target_pairs={{0,24},{8,16},{16,8},{24,0},{1,25},{9,17},{17,9},{25,1},{2,26},{10... | collective-permute-start | bytes 442376 | tf_op jit(solution)/shard_map/ppermute | solution.py:789
  67.6 9.5 %collective-permute-start.13 = (f32[136,256]{1,0:T(8,128)S(1)}, f32[136,256]{1,0:T(8,128)S(1)}, u32[]{:S(2)}, u32[]{:S(2)}) collective-permute-start(f32[136,256]{1,0:T(8,128)S(1)} %shard_map.424.refs_0_), channel_id=1, source_target_pairs={{0,7},{1,6},{2,5},{3,4},{4,3},{5,2},{6,1},{7,0},{8,15},{9,14},{10,... | collective-permute-start | bytes 417800 | tf_op jit(solution)/shard_map/ppermute | solution.py:789
  74.5 2.7 %copy-start.8 = (f32[2,538,256]{2,0,1:T(2,128)S(1)}, f32[2,538,256]{2,0,1:T(2,128)}, u32[]{:S(2)}) copy-start(f32[2,538,256]{2,0,1:T(2,128)} %param.34) | copy-start | bytes 3305476
  74.5 2.7 %copy-start.9 = (f32[2,538,256]{2,0,1:T(2,128)S(1)}, f32[2,538,256]{2,0,1:T(2,128)}, u32[]{:S(2)}) copy-start(f32[2,538,256]{2,0,1:T(2,128)} %param.35) | copy-start | bytes 3305476
  74.5 2.7 %copy-start.19 = (f32[2,257]{1,0:T(2,128)S(1)}, f32[2,257]{1,0:T(2,128)}, u32[]{:S(2)}) copy-start(f32[2,257]{1,0:T(2,128)} %refs_12_.1) | copy-start | bytes 6172
  74.5 2.7 %copy-start.20 = (f32[2,257]{1,0:T(2,128)S(1)}, f32[2,257]{1,0:T(2,128)}, u32[]{:S(2)}) copy-start(f32[2,257]{1,0:T(2,128)} %refs_13_.1) | copy-start | bytes 6172
  (7 other events, 9.1 us)
